TPU v7x, 128 devices: a whole 4x4x4 slice. The times are simulated.
128 devices in a mesh: space: 16 (over z, x), sub: 8 (over y, core).
Axes of the slice: x: 4, y: 4, z: 4, core: 2. Of those that a mesh axis runs over, the one named last changes fastest.
Arguments:
- coords: float32 [3, 16777216], P(None, ('space', 'sub')), may hold values from -1 to 1
- masses: float32 [16777216], P(('space', 'sub')), may hold values from 0.1 to 2
- swap_counts: int32 [128, 3], P(('space', 'sub')), may hold values from 1 to 16384, as said below
- leaf_of_block: int32 [131072], P(('space', 'sub')), may hold values from 0 to 639
- let_send: int32 [128, 128, 32], P(('space', 'sub')), may hold values from 0 to 639
- inter_source: int32 [81920, 189], P(('space', 'sub')), may hold values from 0 to 4735
- inter_offset: int32 [81920, 189], P(('space', 'sub')), may hold values from 0 to 315, as said below
- compress: float32 [216, 64], replicated, may hold values from -0.4375 to 0.4375
- m2l_kernels: bfloat16 [64, 20224], replicated, may hold values from -0.0546875 to 0.0546875
- expand: float32 [64, 216], replicated, may hold values from -0.75 to 0.75
Outputs:
- potential: float32 [16777216], P(('space', 'sub'))
Inputs may be any that keep to these rules, and one draw needn't show every extreme that they name: swap_counts[d, r] equals swap_counts[d XOR k_r, r] of its partner in round r. `inter_offset`: within a row, the 189 offsets are different.
All inputs are finite; a program needn't handle non-finite values.
Results may differ from a plain program's by a relative error of at most 0.003.
Values may be sent and summed in bfloat16 or wider, within the bound.
A program may use at most 192 MiB of HBM per device.

v0:
```python
import jax
import jax.numpy as jnp
from jax import lax
from jax.sharding import PartitionSpec as P

ORDER = 6


def from_partner(block, axis, distance):
    count = lax.axis_size(axis)
    route = []
    for low in range(count):
        high = low | 1 << distance
        if high != low and high < count:
            route += [(low, high), (high, low)]
    return lax.ppermute(block, axis, route)


def cheb_weights(points, order):
    nodes = jnp.cos((2.0 * jnp.arange(order, dtype=jnp.float32) + 1.0) * jnp.pi / (2.0 * order))
    shape_tail = (1,) * points.ndim
    node_prev = jnp.ones((order,), jnp.float32)
    node_cur = nodes
    poly_prev = jnp.ones_like(points)
    poly_cur = points
    total = jnp.full((order,) + points.shape, 1.0 / order, jnp.float32)
    for step in range(1, order):
        total = total + 2.0 / order * node_cur.reshape((order,) + shape_tail) * poly_cur[None]
        node_prev, node_cur = (node_cur, 2.0 * nodes * node_cur - node_prev)
        poly_prev, poly_cur = (poly_cur, 2.0 * points * poly_cur - poly_prev)
    return total


def place_round(stacked, got, rnd, width, limit):
    columns = lax.broadcasted_iota(jnp.int32, (1, width), 1)
    region = stacked[:, rnd * width : (rnd + 1) * width]
    region = jnp.where(columns < limit, got, region)
    return stacked.at[:, rnd * width : (rnd + 1) * width].set(region)


def on_device(
    coords,
    masses,
    swap_counts,
    leaf_of_block,
    let_send,
    inter_source,
    inter_offset,
    compress,
    m2l_kernels,
    expand,
):
    order = ORDER
    nodes_count = compress.shape[0]
    rank = compress.shape[1]
    leaves = inter_source.shape[0]
    inter = inter_source.shape[1]
    offsets_count = m2l_kernels.shape[1] // rank
    local_bodies = coords.shape[1]
    blocks = local_bodies // 128
    width = local_bodies // 8
    stacked = jnp.concatenate([coords, masses[None, :]], axis=0)
    top_bit = lax.axis_size("space").bit_length() - 2
    got_outer = from_partner(stacked[:, 0:width], "space", top_bit)
    got_inner = from_partner(stacked[:, width : 2 * width], "space", 0)
    got_sub = from_partner(stacked[:, 2 * width : 3 * width], "sub", 0)
    stacked = place_round(stacked, got_outer, 0, width, swap_counts[0, 0])
    stacked = place_round(stacked, got_inner, 1, width, swap_counts[0, 1])
    stacked = place_round(stacked, got_sub, 2, width, swap_counts[0, 2])
    weights = cheb_weights(stacked[:3], order)
    onehot_leaf = (
        leaf_of_block[None, :] == lax.broadcasted_iota(jnp.int32, (leaves, 1), 0)
    ).astype(jnp.float32)
    weight_z = weights[:, 2].reshape(order, blocks, 128)
    pair_mass = (
        (weights[:, 0] * stacked[3][None, :])[:, None, :] * weights[:, 1][None, :, :]
    ).reshape(order * order, blocks, 128)
    node_sums = jnp.stack(
        [jnp.sum(pair_mass * weight_z[k][None], axis=2) for k in range(order)], axis=1
    )
    node_sums = node_sums.reshape(nodes_count, blocks)
    multipole = lax.dot_general(
        onehot_leaf,
        node_sums,
        (((1,), (1,)), ((), ())),
        precision=lax.Precision.HIGHEST,
        preferred_element_type=jnp.float32,
    )
    coeffs = jnp.dot(
        multipole, compress, precision=lax.Precision.HIGHEST, preferred_element_type=jnp.float32
    ).astype(jnp.bfloat16)
    send_ids = let_send[0]
    peers = send_ids.shape[0]
    per_peer = send_ids.shape[1]
    outgoing = multipole[send_ids].reshape(peers, per_peer * nodes_count)
    incoming = lax.all_to_all(outgoing, ("space", "sub"), split_axis=0, concat_axis=0, tiled=True)
    ghosts = jnp.dot(
        incoming.reshape(peers * per_peer, nodes_count),
        compress,
        precision=lax.Precision.HIGHEST,
        preferred_element_type=jnp.float32,
    ).astype(jnp.bfloat16)
    table = jnp.concatenate([coeffs, ghosts], axis=0)
    target_rows = 128
    target_blocks = leaves // target_rows
    offset_ids = lax.broadcasted_iota(jnp.int32, (1, offsets_count, 1), 1)

    def translate_block(pack):
        sources, offsets = pack
        gathered = table[sources]
        selector = (offsets[:, None, :] == offset_ids).astype(jnp.bfloat16)
        placed = lax.dot_general(
            selector, gathered, (((2,), (1,)), ((0,), (0,))), preferred_element_type=jnp.float32
        )
        placed = placed.astype(jnp.bfloat16).reshape(target_rows, offsets_count * rank)
        return lax.dot_general(
            placed, m2l_kernels, (((1,), (1,)), ((), ())), preferred_element_type=jnp.float32
        )

    compressed_local = lax.map(
        translate_block,
        (
            inter_source.reshape(target_blocks, target_rows, inter),
            inter_offset.reshape(target_blocks, target_rows, inter),
        ),
    )
    compressed_local = compressed_local.reshape(leaves, rank)
    local_nodes = jnp.dot(
        compressed_local,
        expand,
        precision=lax.Precision.HIGHEST,
        preferred_element_type=jnp.float32,
    )
    node_columns = lax.dot_general(
        local_nodes,
        onehot_leaf,
        (((0,), (0,)), ((), ())),
        precision=lax.Precision.HIGHEST,
        preferred_element_type=jnp.float32,
    )
    node_columns = node_columns.reshape(order * order, order, blocks)
    inner = node_columns[:, 0, :, None] * weight_z[0][None]
    for k in range(1, order):
        inner = inner + node_columns[:, k, :, None] * weight_z[k][None]
    pair_plain = (weights[:, 0][:, None, :] * weights[:, 1][None, :, :]).reshape(
        order * order, blocks, 128
    )
    values = jnp.sum(pair_plain * inner, axis=0)
    return values.reshape(local_bodies)


def solution(mesh):
    return jax.shard_map(
        on_device,
        mesh=mesh,
        in_specs=(
            P(None, ("space", "sub")),
            P(("space", "sub")),
            P(("space", "sub"), None),
            P(("space", "sub")),
            P(("space", "sub"), None, None),
            P(("space", "sub"), None),
            P(("space", "sub"), None),
            P(),
            P(),
            P(),
        ),
        out_specs=P(("space", "sub")),
        check_vma=False,
    )
```

profile of v0, /device:TPU:1, one launch (start us, length us, event | category | flops | bytes accessed | tf_op | source)
XLA Modules:
  0.0 727.1 jit_solution(5814294326561483065)
XLA Ops:
  20.8 8.6 %multiply_add_fusion = f32[6,3,131072]{2,1,0:T(4,128)S(1)} fusion(f32[3,131072]{1,0:T(4,128)S(1)} %get-tuple-element.153, f32[6]{0:T(128)S(1)} %get-tuple-element.163, f32[3,131072]{1,0:T(4,128)S(1)} %get-tuple-element.150, f32[6]{0:T(128)S(1)} %get-tuple-element.164, f32[3,131072]{1,0:T(4,128)S(1)} %get-tuple-element.152, f32[6]{0:T(128)S(1)} %get-tuple-element.165, ...), kind=kLoop, calls=%fused_computation.19 | loop fusion | flops 23592960 | bytes 17301624 | tf_op jit(solution)/shard_map/add | solution.py:28
  46.1 16.4 %broadcast_multiply_fusion = (f32[6,6,131072]{2,1,0:T(8,128)}, f32[6,6,131072]{2,1,0:T(8,128)}) fusion(f32[6,131072]{1,0:T(8,128)S(1)} %bitcast.98, f32[6,131072]{1,0:T(8,128)S(1)} %bitcast.99, f32[6,131072]{1,0:T(8,128)S(1)} %bitcast.100), kind=kLoop, calls=%fused_computation.17 | loop fusion | flops 9437184 | bytes 47185920 | tf_op jit(solution)/shard_map/mul | solution.py:76
  62.5 19.2 %mul.501 = f32[36,1024,128]{2,1,0:T(8,128)} reshape(f32[6,6,131072]{2,1,0:T(8,128)} %get-tuple-element.144) | data formatting | bytes 37748736 | tf_op jit(solution)/shard_map/mul | solution.py:76
  81.8 31.9 %multiply_reduce_fusion.1 = (f32[36,1024]{1,0:T(8,128)S(1)}, f32[36,1024]{1,0:T(8,128)S(1)}, f32[36,1024]{1,0:T(8,128)S(1)}, f32[36,1024]{1,0:T(8,128)S(1)}, f32[36,1024]{1,0:T(8,128)S(1)}, /*index=5*/f32[36,1024]{1,0:T(8,128)S(1)}) fusion(f32[36,1024,128]{2,1,0:T(8,128)} %mul.501, f32[1024,128]{1,0:T(8,128)S(1)} %bitcast.103, f32[1024,128]{1,0:T(8,128)S(1)} %bitcast.105, ...), kind=kLoop, calls=%fused_computation.11 | loop fusion | flops 56401920 | bytes 22904832 | tf_op jit(solution)/shard_map/reduce_sum | solution.py:79
  116.3 16.1 %gather_fusion.1 = f32[4096,216]{1,0:T(8,128)} fusion(f32[640,216]{1,0:T(8,128)S(1)} %copy.42, s32[4096]{0:T(1024)S(1)} %broadcast_clamp_fusion), kind=kCustom, calls=%fused_computation.1 | custom fusion | bytes 7094272 | tf_op jit(solution)/shard_map/gather | solution.py:95
  132.4 9.9 %all_to_all.8 = f32[128,1,6912]{2,1,0:T(1,128)} reshape(f32[4096,216]{1,0:T(8,128)} %gather_fusion.1) | data formatting | bytes 7077888 | tf_op jit(solution)/shard_map/all_to_all | solution.py:96
  142.3 9.2 %all-to-all-start = ((f32[128,1,6912]{2,1,0:T(1,128)}), f32[128,1,6912]{2,1,0:T(1,128)}, u32[]{:S(2)}, u32[]{:S(2)}) async-start(f32[128,1,6912]{2,1,0:T(1,128)} %all_to_all.8), calls=%async_computation | async-start | bytes 7077888 | tf_op jit(solution)/shard_map/all_to_all | solution.py:96
  152.0 19.3 %mul.495 = f32[36,1024,128]{2,1,0:T(8,128)} reshape(f32[6,6,131072]{2,1,0:T(8,128)} %get-tuple-element.145) | data formatting | bytes 37748736 | tf_op jit(solution)/shard_map/mul | solution.py:145
  171.8 25.5 %all-to-all-done = f32[128,1,6912]{2,1,0:T(1,128)} async-done(((f32[128,1,6912]{2,1,0:T(1,128)}), f32[128,1,6912]{2,1,0:T(1,128)}, u32[]{:S(2)}, u32[]{:S(2)}) %all-to-all-start) | async-done | bytes 3538976 | tf_op jit(solution)/shard_map/all_to_all | solution.py:96
  197.3 37.1 %reduce.25 = f32[128,6912]{1,0:T(8,128)} reduce(f32[128,1,6912]{2,1,0:T(1,128)} %all-to-all-done, f32[]{:T(128)} %constant.126), dimensions={1}, to_apply=%all_to_all.7.reduce_sub_computation | reduce | bytes 7077892 | tf_op jit(solution)/shard_map/all_to_all | solution.py:96
  250.4 430.7 %while.14 = (s32[]{:T(128)}, f32[5,128,64]{1,0,2:T(8,128)}, s32[5,128,189]{2,1,0:T(8,128)S(1)}, s32[5,128,189]{2,1,0:T(8,128)S(1)}, bf16[4736,64]{1,0:T(8,128)(2...) while((s32[]{:T(128)}, f32[5,128,64]{1,0,2:T(8,128)}, ...), condition=%wide.region_10.11_spmd.clone, body=%wide.region_9.10_spmd.clone.sunk | while | flops 1320198528 | bytes 39848552 | solution.py:120
  251.0 49.4 %gather_fusion = bf16[24192,64]{1,0:T(8,128)(2,1)} fusion(bf16[4736,64]{1,0:T(8,128)(2,1)S(1)} %get-tuple-element.224, s32[24576]{0:T(1024)S(1)} %pad_clamp_fusion.2), kind=kCustom, calls=%fused_computation.clone.clone.1 | custom fusion | bytes 6289920 | tf_op jit(solution)/shard_map/while/body/eval_jaxpr/gather | solution.py:110
  300.4 8.3 %reshape.359 = bf16[128,189,64]{2,1,0:T(8,128)(2,1)} reshape(bf16[24192,64]{1,0:T(8,128)(2,1)} %gather_fusion) | data formatting | bytes 6193152 | tf_op jit(solution)/shard_map/while/body/eval_jaxpr/gather | solution.py:110
  308.7 12.6 %fusion.45 = bf16[128,316,64]{1,2,0:T(8,128)(2,1)} fusion(bf16[128,189,64]{2,1,0:T(8,128)(2,1)} %reshape.359, s32[128,189]{1,0:T(8,128)S(1)} %dynamic-slice_bitcast_fusion.2), kind=kOutput, calls=%fused_computation.6.clone.1 | convolution fusion | flops 988751360 | bytes 8370688 | tf_op jit(solution)/shard_map/while/body/eval_jaxpr/dot_general | solution.py:112
  321.2 9.4 %copy.90 = bf16[128,316,64]{0,2,1:T(8,128)(2,1)} copy(bf16[128,316,64]{1,2,0:T(8,128)(2,1)} %fusion.45) | data formatting | bytes 10354688 | tf_op jit(solution)/shard_map/while/body/eval_jaxpr/convert_element_type | solution.py:115
  337.1 49.4 %gather_fusion = bf16[24192,64]{1,0:T(8,128)(2,1)} fusion(bf16[4736,64]{1,0:T(8,128)(2,1)S(1)} %get-tuple-element.224, s32[24576]{0:T(1024)S(1)} %pad_clamp_fusion.2), kind=kCustom, calls=%fused_computation.clone.clone.1 | custom fusion | bytes 6289920 | tf_op jit(solution)/shard_map/while/body/eval_jaxpr/gather | solution.py:110
  386.5 8.3 %reshape.359 = bf16[128,189,64]{2,1,0:T(8,128)(2,1)} reshape(bf16[24192,64]{1,0:T(8,128)(2,1)} %gather_fusion) | data formatting | bytes 6193152 | tf_op jit(solution)/shard_map/while/body/eval_jaxpr/gather | solution.py:110
  394.8 12.5 %fusion.45 = bf16[128,316,64]{1,2,0:T(8,128)(2,1)} fusion(bf16[128,189,64]{2,1,0:T(8,128)(2,1)} %reshape.359, s32[128,189]{1,0:T(8,128)S(1)} %dynamic-slice_bitcast_fusion.2), kind=kOutput, calls=%fused_computation.6.clone.1 | convolution fusion | flops 988751360 | bytes 8370688 | tf_op jit(solution)/shard_map/while/body/eval_jaxpr/dot_general | solution.py:112
  407.3 9.4 %copy.90 = bf16[128,316,64]{0,2,1:T(8,128)(2,1)} copy(bf16[128,316,64]{1,2,0:T(8,128)(2,1)} %fusion.45) | data formatting | bytes 10354688 | tf_op jit(solution)/shard_map/while/body/eval_jaxpr/convert_element_type | solution.py:115
  423.2 49.4 %gather_fusion = bf16[24192,64]{1,0:T(8,128)(2,1)} fusion(bf16[4736,64]{1,0:T(8,128)(2,1)S(1)} %get-tuple-element.224, s32[24576]{0:T(1024)S(1)} %pad_clamp_fusion.2), kind=kCustom, calls=%fused_computation.clone.clone.1 | custom fusion | bytes 6289920 | tf_op jit(solution)/shard_map/while/body/eval_jaxpr/gather | solution.py:110
  472.6 8.3 %reshape.359 = bf16[128,189,64]{2,1,0:T(8,128)(2,1)} reshape(bf16[24192,64]{1,0:T(8,128)(2,1)} %gather_fusion) | data formatting | bytes 6193152 | tf_op jit(solution)/shard_map/while/body/eval_jaxpr/gather | solution.py:110
  480.9 12.6 %fusion.45 = bf16[128,316,64]{1,2,0:T(8,128)(2,1)} fusion(bf16[128,189,64]{2,1,0:T(8,128)(2,1)} %reshape.359, s32[128,189]{1,0:T(8,128)S(1)} %dynamic-slice_bitcast_fusion.2), kind=kOutput, calls=%fused_computation.6.clone.1 | convolution fusion | flops 988751360 | bytes 8370688 | tf_op jit(solution)/shard_map/while/body/eval_jaxpr/dot_general | solution.py:112
  493.4 9.4 %copy.90 = bf16[128,316,64]{0,2,1:T(8,128)(2,1)} copy(bf16[128,316,64]{1,2,0:T(8,128)(2,1)} %fusion.45) | data formatting | bytes 10354688 | tf_op jit(solution)/shard_map/while/body/eval_jaxpr/convert_element_type | solution.py:115
  509.3 49.4 %gather_fusion = bf16[24192,64]{1,0:T(8,128)(2,1)} fusion(bf16[4736,64]{1,0:T(8,128)(2,1)S(1)} %get-tuple-element.224, s32[24576]{0:T(1024)S(1)} %pad_clamp_fusion.2), kind=kCustom, calls=%fused_computation.clone.clone.1 | custom fusion | bytes 6289920 | tf_op jit(solution)/shard_map/while/body/eval_jaxpr/gather | solution.py:110
  558.7 8.3 %reshape.359 = bf16[128,189,64]{2,1,0:T(8,128)(2,1)} reshape(bf16[24192,64]{1,0:T(8,128)(2,1)} %gather_fusion) | data formatting | bytes 6193152 | tf_op jit(solution)/shard_map/while/body/eval_jaxpr/gather | solution.py:110
  567.0 12.6 %fusion.45 = bf16[128,316,64]{1,2,0:T(8,128)(2,1)} fusion(bf16[128,189,64]{2,1,0:T(8,128)(2,1)} %reshape.359, s32[128,189]{1,0:T(8,128)S(1)} %dynamic-slice_bitcast_fusion.2), kind=kOutput, calls=%fused_computation.6.clone.1 | convolution fusion | flops 988751360 | bytes 8370688 | tf_op jit(solution)/shard_map/while/body/eval_jaxpr/dot_general | solution.py:112
  579.5 9.4 %copy.90 = bf16[128,316,64]{0,2,1:T(8,128)(2,1)} copy(bf16[128,316,64]{1,2,0:T(8,128)(2,1)} %fusion.45) | data formatting | bytes 10354688 | tf_op jit(solution)/shard_map/while/body/eval_jaxpr/convert_element_type | solution.py:115
  595.4 49.4 %gather_fusion = bf16[24192,64]{1,0:T(8,128)(2,1)} fusion(bf16[4736,64]{1,0:T(8,128)(2,1)S(1)} %get-tuple-element.224, s32[24576]{0:T(1024)S(1)} %pad_clamp_fusion.2), kind=kCustom, calls=%fused_computation.clone.clone.1 | custom fusion | bytes 6289920 | tf_op jit(solution)/shard_map/while/body/eval_jaxpr/gather | solution.py:110
  644.8 8.3 %reshape.359 = bf16[128,189,64]{2,1,0:T(8,128)(2,1)} reshape(bf16[24192,64]{1,0:T(8,128)(2,1)} %gather_fusion) | data formatting | bytes 6193152 | tf_op jit(solution)/shard_map/while/body/eval_jaxpr/gather | solution.py:110
  653.0 12.5 %fusion.45 = bf16[128,316,64]{1,2,0:T(8,128)(2,1)} fusion(bf16[128,189,64]{2,1,0:T(8,128)(2,1)} %reshape.359, s32[128,189]{1,0:T(8,128)S(1)} %dynamic-slice_bitcast_fusion.2), kind=kOutput, calls=%fused_computation.6.clone.1 | convolution fusion | flops 988751360 | bytes 8370688 | tf_op jit(solution)/shard_map/while/body/eval_jaxpr/dot_general | solution.py:112
  665.6 9.4 %copy.90 = bf16[128,316,64]{0,2,1:T(8,128)(2,1)} copy(bf16[128,316,64]{1,2,0:T(8,128)(2,1)} %fusion.45) | data formatting | bytes 10354688 | tf_op jit(solution)/shard_map/while/body/eval_jaxpr/convert_element_type | solution.py:115
  692.9 34.1 %multiply_reduce_fusion = f32[1024,128]{1,0:T(8,128)} fusion(f32[36,1024,128]{2,1,0:T(8,128)} %mul.495, f32[36,1024]{1,0:T(8,128)S(1)} %bitcast.120, f32[36,1024]{1,0:T(8,128)S(1)} %bitcast.121, f32[36,1024]{1,0:T(8,128)S(1)} %bitcast.122, f32[36,1024]{1,0:T(8,128)S(1)} %bitcast.123, f32[36,1024]{1,0:T(8,128)S(1)} %bitcast.124, f32[36,1024]{1,0:T(8,128)S(1)} %bitcast.119, ...), kind=kLoop, calls=%fused_computation.10 | loop fusion | flops 61210624 | bytes 23429120 | tf_op jit(solution)/shard_map/reduce_sum | solution.py:148
  (132 shorter events, 100.8 us)
Async XLA Ops:
  0.0 171.3 %copy-start = (f32[216,64]{0,1:T(8,128)S(1)}, f32[216,64]{0,1:T(8,128)}, u32[]{:S(2)}) copy-start(f32[216,64]{0,1:T(8,128)} %param.25) | copy-start | bytes 165892
  0.0 11.5 %copy-start.18 = (s32[1,3]{1,0:T(1,128)S(1)}, s32[1,3]{1,0:T(1,128)}, u32[]{:S(2)}) copy-start(s32[1,3]{1,0:T(1,128)} %param.20) | copy-start | bytes 40
  0.0 14.0 %copy-start.17 = (s32[1,128,32]{1,2,0:T(8,128)S(1)}, s32[1,128,32]{1,2,0:T(8,128)}, u32[]{:S(2)}) copy-start(s32[1,128,32]{1,2,0:T(8,128)} %param.22) | copy-start | bytes 49156
  2.3 15.4 %collective-permute-start.2 = (f32[4,16384]{1,0:T(4,128)}, f32[4,16384]{1,0:T(4,128)S(1)}, u32[]{:S(2)}, u32[]{:S(2)}) collective-permute-start(f32[4,16384]{1,0:T(4,128)} %get-tuple-element.146), channel_id=1, source_target_pairs={{0,1},{1,0},{2,3},{3,2},{4,5},{5,4},{6,7},{7,6},{8,9},{9,8},{10,11... | collective-permute-start | bytes 786440 | tf_op jit(solution)/shard_map/ppermute | solution.py:16
  3.7 13.2 %collective-permute-start.1 = (f32[4,16384]{1,0:T(4,128)}, f32[4,16384]{1,0:T(4,128)S(1)}, u32[]{:S(2)}, u32[]{:S(2)}) collective-permute-start(f32[4,16384]{1,0:T(4,128)} %get-tuple-element.148), channel_id=1, source_target_pairs={{0,8},{8,0},{16,24},{24,16},{32,40},{40,32},{48,56},{56,48},{64,72... | collective-permute-start | bytes 786440 | tf_op jit(solution)/shard_map/ppermute | solution.py:16
  5.0 11.2 %collective-permute-start = (f32[4,16384]{1,0:T(4,128)S(1)}, f32[4,16384]{1,0:T(4,128)S(1)}, u32[]{:S(2)}, u32[]{:S(2)}) collective-permute-start(f32[4,16384]{1,0:T(4,128)S(1)} %get-tuple-element.147), channel_id=1, source_target_pairs={{0,64},{64,0},{8,72},{72,8},{16,80},{80,16},{24,88},{88,24},{32,96... | collective-permute-start | bytes 786440 | tf_op jit(solution)/shard_map/ppermute | solution.py:16
  32.7 49.1 %copy-start.2 = (f32[1,1,131072]{2,1,0:T(1,128)}, f32[1,1,131072]{2,1,0:T(1,128)S(1)}, u32[]{:S(2)}) copy-start(f32[1,1,131072]{2,1,0:T(1,128)S(1)} %get-tuple-element.135) | copy-start | bytes 1572868
  32.7 49.1 %copy-start.4 = (f32[1,1,131072]{2,1,0:T(1,128)}, f32[1,1,131072]{2,1,0:T(1,128)S(1)}, u32[]{:S(2)}) copy-start(f32[1,1,131072]{2,1,0:T(1,128)S(1)} %get-tuple-element.136) | copy-start | bytes 1572868
  32.7 49.0 %copy-start.6 = (f32[1,1,131072]{2,1,0:T(1,128)}, f32[1,1,131072]{2,1,0:T(1,128)S(1)}, u32[]{:S(2)}) copy-start(f32[1,1,131072]{2,1,0:T(1,128)S(1)} %get-tuple-element.137) | copy-start | bytes 1572868
  32.7 49.0 %copy-start.8 = (f32[1,1,131072]{2,1,0:T(1,128)}, f32[1,1,131072]{2,1,0:T(1,128)S(1)}, u32[]{:S(2)}) copy-start(f32[1,1,131072]{2,1,0:T(1,128)S(1)} %get-tuple-element.138) | copy-start | bytes 1572868
  32.7 49.0 %copy-start.10 = (f32[1,1,131072]{2,1,0:T(1,128)}, f32[1,1,131072]{2,1,0:T(1,128)S(1)}, u32[]{:S(2)}) copy-start(f32[1,1,131072]{2,1,0:T(1,128)S(1)} %get-tuple-element.139) | copy-start | bytes 1572868
  32.7 49.0 %copy-start.12 = (f32[1,1,131072]{2,1,0:T(1,128)}, f32[1,1,131072]{2,1,0:T(1,128)S(1)}, u32[]{:S(2)}) copy-start(f32[1,1,131072]{2,1,0:T(1,128)S(1)} %get-tuple-element.140) | copy-start | bytes 1572868
  113.7 0.8 copy-start.19
  142.3 9.2 %copy-start.14 = (s32[640,189]{0,1:T(8,128)S(1)}, s32[640,189]{0,1:T(8,128)}, u32[]{:S(2)}) copy-start(s32[640,189]{0,1:T(8,128)} %param.23) | copy-start | bytes 1451524
  142.3 9.4 %copy-start.15 = (s32[640,189]{0,1:T(8,128)S(1)}, s32[640,189]{0,1:T(8,128)}, u32[]{:S(2)}) copy-start(s32[640,189]{0,1:T(8,128)} %param.24) | copy-start | bytes 1451524
  142.3 55.0 %all-to-all-start = ((f32[128,1,6912]{2,1,0:T(1,128)}), f32[128,1,6912]{2,1,0:T(1,128)}, u32[]{:S(2)}, u32[]{:S(2)}) async-start(f32[128,1,6912]{2,1,0:T(1,128)} %all_to_all.8), calls=%async_computation | async-start | bytes 7077888 | tf_op jit(solution)/shard_map/all_to_all | solution.py:96
  250.4 430.7 %copy-start.16 = (f32[64,216]{1,0:T(8,128)S(1)}, f32[64,216]{1,0:T(8,128)}, u32[]{:S(2)}) copy-start(f32[64,216]{1,0:T(8,128)} %param.27) | copy-start | bytes 165892
  250.4 432.5 %copy-start.20 = (s32[1024]{0:T(1024)S(1)}, s32[1024]{0:T(1024)}, u32[]{:S(2)}) copy-start(s32[1024]{0:T(1024)} %param.21) | copy-start | bytes 12292
  681.0 11.8 %copy-start.3 = (f32[1,1,131072]{2,1,0:T(1,128)S(1)}, f32[1,1,131072]{2,1,0:T(1,128)}, u32[]{:S(2)}) copy-start(f32[1,1,131072]{2,1,0:T(1,128)} %copy-done.2) | copy-start | bytes 1572868
  681.0 11.8 %copy-start.5 = (f32[1,1,131072]{2,1,0:T(1,128)S(1)}, f32[1,1,131072]{2,1,0:T(1,128)}, u32[]{:S(2)}) copy-start(f32[1,1,131072]{2,1,0:T(1,128)} %copy-done.4) | copy-start | bytes 1572868
  681.0 11.8 %copy-start.7 = (f32[1,1,131072]{2,1,0:T(1,128)S(1)}, f32[1,1,131072]{2,1,0:T(1,128)}, u32[]{:S(2)}) copy-start(f32[1,1,131072]{2,1,0:T(1,128)} %copy-done.6) | copy-start | bytes 1572868
  681.0 11.8 %copy-start.9 = (f32[1,1,131072]{2,1,0:T(1,128)S(1)}, f32[1,1,131072]{2,1,0:T(1,128)}, u32[]{:S(2)}) copy-start(f32[1,1,131072]{2,1,0:T(1,128)} %copy-done.8) | copy-start | bytes 1572868
  681.1 11.8 %copy-start.11 = (f32[1,1,131072]{2,1,0:T(1,128)S(1)}, f32[1,1,131072]{2,1,0:T(1,128)}, u32[]{:S(2)}) copy-start(f32[1,1,131072]{2,1,0:T(1,128)} %copy-done.10) | copy-start | bytes 1572868
  681.1 11.8 %copy-start.13 = (f32[1,1,131072]{2,1,0:T(1,128)S(1)}, f32[1,1,131072]{2,1,0:T(1,128)}, u32[]{:S(2)}) copy-start(f32[1,1,131072]{2,1,0:T(1,128)} %copy-done.12) | copy-start | bytes 1572868
  692.9 34.1 %copy-start.1 = (f32[216,64]{0,1:T(8,128)S(1)}, f32[216,64]{0,1:T(8,128)}, u32[]{:S(2)}) copy-start(f32[216,64]{0,1:T(8,128)} %param.25) | copy-start | bytes 165892
where the time goes:
time: 737 us; the launch traced here: 727 us
  local copies, waits for them, and re-layouts  439 us (60%)
  other arithmetic  149 us (20%)
  matrix products  97 us (13%)
  waiting for transfers between devices  25.6 us (3%)
  starting transfers between devices  15.5 us (2%)
    gather x10, local copies, waits for them, and re-layouts, translate_block(): gathered = table[sources]  288 us
    dot_general x5, matrix products, translate_block(): lax.dot_general(selector, gathered, (((2,), (1,)), ((0,), (0,))), preferr...  62.8 us
    convert_element_type x5, local copies, waits for them, and re-layouts, translate_block(): placed.astype(jnp.bfloat16).reshape(target_rows, offsets_count * rank)  46.8 us
    all_to_all x1, other arithmetic, on_device(): lax.all_to_all(outgoing, ('space', 'sub'), split_axis=0, concat_axis=0, t...  37.1 us
    reduce_sum x1, other arithmetic, on_device(): values = jnp.sum(pair_plain * inner, axis=0)  34.1 us
    reduce_sum x1, other arithmetic, on_device(): jnp.sum(pair_mass * weight_z[k][None], axis=2)  31.9 us
    all_to_all x1, waiting for transfers between devices, on_device(): lax.all_to_all(outgoing, ('space', 'sub'), split_axis=0, concat_axis=0, t...  25.5 us
    dot_general x5, matrix products, translate_block(): lax.dot_general(placed, m2l_kernels, (((1,), (1,)), ((), ())), preferred_...  21.6 us
  transfers between devices with their start and end apart: 4, of which 1 were waited for; matrix products, arithmetic and copies ran while one was open for 4% of the time, Pallas kernels for 0%

commit v1 on v0

v1 whole, which is shorter than its diff:
```python
import functools

import jax
import jax.numpy as jnp
import numpy as np
from jax import lax
from jax.experimental import pallas as pl
from jax.experimental.pallas import tpu as pltpu
from jax.sharding import PartitionSpec as P

ORDER = 6
RANK = 64
BLOCK = 128
REGION = 128
SWAPS = 3
GROUP = 80
SLOTS = 192
PAIRS = 160
PITCH = 81
UNROLL = 4


def params(**more):
    return pltpu.CompilerParams(vmem_limit_bytes=56 << 20, **more)


def from_partner(block, axis, distance):
    count = lax.axis_size(axis)
    route = []
    for low in range(count):
        high = low | 1 << distance
        if high != low and high < count:
            route += [(low, high), (high, low)]
    return lax.ppermute(block, axis, route)


def node_weights(points):
    twice = 2.0 * points
    polys = [None, points, twice * points - 1.0]
    for _ in range(3):
        polys.append(twice * polys[-1] - polys[-2])
    weights = [None] * ORDER
    for j in range(ORDER // 2):
        c = [np.float32(np.cos(k * (2 * j + 1) * np.pi / (2 * ORDER)) / 3.0) for k in range(ORDER)]
        even = np.float32(1.0 / ORDER) + c[2] * polys[2] + c[4] * polys[4]
        odd = c[1] * polys[1] + c[3] * polys[3] + c[5] * polys[5]
        weights[j] = even + odd
        weights[ORDER - 1 - j] = even - odd
    return weights


def split_three(values):
    first = values.astype(jnp.bfloat16)
    rest = values - first.astype(jnp.float32)
    second = rest.astype(jnp.bfloat16)
    third = (rest - second.astype(jnp.float32)).astype(jnp.bfloat16)
    return first, second, third


def gather_moments(bodies, out_ref, wx, wy, wz):
    mass = bodies[3].T
    for j, weight in enumerate(node_weights(bodies[0].T)):
        wx[j] = weight * mass
    for scratch, dim in ((wy, 1), (wz, 2)):
        for j, weight in enumerate(node_weights(bodies[dim].T)):
            scratch[j] = weight

    def along(i, carry):
        def chunk(v, sums):
            at = pl.ds(pl.multiple_of(v * 8, 8), 8)
            left = wx[i, at, :]
            inner = [wz[k, at, :] for k in range(ORDER)]
            new = []
            for j in range(ORDER):
                pair = left * wy[j, at, :]
                for k in range(ORDER):
                    new.append(sums[j * ORDER + k] + pair * inner[k])
            return tuple(new)

        zero = jnp.zeros((8, REGION), jnp.float32)
        sums = lax.fori_loop(0, BLOCK // 8, chunk, (zero,) * (ORDER * ORDER), unroll=4)
        for n in range(ORDER * ORDER):
            out_ref[pl.ds(i * ORDER * ORDER + n, 1), :] = jnp.sum(sums[n], axis=0, keepdims=True)
        return carry

    lax.fori_loop(0, ORDER, along, 0)


def moments_kernel(bodies_ref, out_ref, wx, wy, wz):
    gather_moments(bodies_ref, out_ref, wx, wy, wz)


def swapped_moments_kernel(counts_ref, bodies_ref, got0_ref, got1_ref, got2_ref, out_ref, merged_ref, wx, wy, wz):
    column = lax.broadcasted_iota(jnp.int32, (REGION, BLOCK), 0) * BLOCK + lax.broadcasted_iota(
        jnp.int32, (REGION, BLOCK), 1
    )
    for rnd, got in enumerate((got0_ref, got1_ref, got2_ref)):

        @pl.when(pl.program_id(0) == rnd)
        def _():
            keep = column < counts_ref[rnd]
            for dim in range(4):
                merged_ref[dim] = jnp.where(keep, got[dim], bodies_ref[dim])

    gather_moments(merged_ref, out_ref, wx, wy, wz)


def weight_scratch():
    return [pltpu.VMEM((ORDER, BLOCK, REGION), jnp.float32) for _ in range(3)]


def coefficients_kernel(send_ref, swapped_ref, stayed_ref, leaf_ref, compress_ref, own_ref, out_ref, padded):
    leaves = own_ref.shape[0]
    peers = out_ref.shape[0] // 16
    total = jnp.zeros((leaves, 2 * RANK), jnp.float32)
    at = 0
    for sums in (swapped_ref, stayed_ref):
        count = sums.shape[1]
        ids = leaf_ref[:, pl.ds(at, count)]
        onehot = lax.broadcasted_iota(jnp.int32, (leaves, count), 0) == ids
        onehot = jnp.where(onehot, 1.0, 0.0).astype(jnp.bfloat16)
        moved = jnp.dot(
            compress_ref[...], sums[...], precision=lax.Precision.HIGHEST, preferred_element_type=jnp.float32
        )
        for part in split_three(moved):
            total += lax.dot_general(onehot, part, (((1,), (1,)), ((), ())), preferred_element_type=jnp.float32)
        at += count
    own = total.astype(jnp.bfloat16).astype(jnp.float32)
    own_ref[...] = own
    padded[pl.ds(0, 8), :] = jnp.zeros((8, 2 * RANK), jnp.float32)
    padded[pl.ds(8, leaves), :] = own
    padded[pl.ds(8 + leaves, 8), :] = jnp.zeros((8, 2 * RANK), jnp.float32)
    row_of = lax.broadcasted_iota(jnp.int32, (8, 2 * RANK), 0)
    low = lax.broadcasted_iota(jnp.int32, (8, 2 * RANK), 1) < RANK

    def pack(peer, carry):
        line = send_ref.at[pl.ds(peer * 32, 32)]
        halves = []
        for start in (0, 8):
            rows = None
            for j in range(8):
                slot = 2 * (start + j)
                both = jnp.where(low, padded[pl.ds(line[slot], 8), :], padded[pl.ds(line[slot + 1], 8), :])
                rows = both if rows is None else jnp.where(row_of == j, both, rows)
            halves.append(rows)
        out_ref[pl.ds(pl.multiple_of(peer * 16, 16), 16), :] = jnp.concatenate(halves, axis=0).astype(jnp.bfloat16)
        return carry

    lax.fori_loop(0, peers, pack, 0, unroll=4)


def translate_kernel(leaves, inter, src_ref, off_ref, own_ref, ghost_ref, kernels_ref, out_ref, tab, iota, held, placed, m2l_ref, sem):
    step = pl.program_id(0)
    last = pl.num_programs(0) - 1
    rows = (tab.shape[0] - 16) // 2
    ghosts = ghost_ref.shape[0]

    @pl.when(step == 0)
    def _():
        width = kernels_ref.shape[1]
        copy = pltpu.make_async_copy(kernels_ref, m2l_ref.at[:, pl.ds(0, width)], sem)
        copy.start()
        m2l_ref[:, pl.ds(width, m2l_ref.shape[1] - width)] = jnp.zeros(
            (m2l_ref.shape[0], m2l_ref.shape[1] - width), jnp.bfloat16
        )
        iota[...] = lax.broadcasted_iota(jnp.int32, iota.shape, 0).astype(jnp.float32).astype(jnp.bfloat16)
        held[...] = jnp.zeros_like(held)
        tab[pl.ds(0, 8), :] = jnp.zeros((8, 128), jnp.float32)
        tab[pl.ds(2 * rows + 8, 8), :] = jnp.zeros((8, 128), jnp.float32)
        low = lax.broadcasted_iota(jnp.int32, (leaves, 128), 1) < 64
        own = own_ref[...]
        tab[pl.ds(8, leaves), :] = jnp.where(low, own, 0.0)
        tab[pl.ds(8 + rows, leaves), :] = jnp.where(low, 0.0, own)
        low = lax.broadcasted_iota(jnp.int32, (ghosts, 128), 1) < 64
        got = ghost_ref[...].astype(jnp.float32)
        turned = pltpu.roll(got, 64, 1)
        tab[pl.ds(8 + leaves, ghosts), :] = jnp.where(low, got, 0.0)
        tab[pl.ds(8 + leaves + ghosts, ghosts), :] = jnp.where(low, turned, 0.0)
        tab[pl.ds(8 + rows + leaves, ghosts), :] = jnp.where(low, 0.0, turned)
        tab[pl.ds(8 + rows + leaves + ghosts, ghosts), :] = jnp.where(low, 0.0, got)
        copy.wait()

    now = lax.rem(step, 2) * (PAIRS * PITCH)
    before = lax.rem(step + 1, 2) * (PAIRS * PITCH)
    lane_of = lax.broadcasted_iota(jnp.int32, (8, 128), 0)

    def collect(cells, slots):
        lines = [src_ref.at[pl.ds(cell * SLOTS, SLOTS)] for cell in cells]
        for pack in range(SLOTS // 16):
            parts = [[] for _ in cells]
            for start in (pack * 16, pack * 16 + 8):
                totals = [None] * len(cells)
                for j in range(min(8, inter - start)):
                    for u, line in enumerate(lines):
                        window = tab[pl.ds(line[start + j], 8), :]
                        totals[u] = window if j == 0 else jnp.where(lane_of == j, window, totals[u])
                for u in range(len(cells)):
                    parts[u].append(totals[u])
            for u, slot in enumerate(slots):
                held[slot, pl.ds(pack * 16, 16), :] = jnp.concatenate(parts[u], axis=0).astype(jnp.bfloat16)

    def pick(cell, rows_of):
        line = jnp.broadcast_to(off_ref[pl.ds(cell, 1), :], (16, 256)).astype(jnp.bfloat16)
        line = jnp.concatenate([line] * (PAIRS // 16), axis=0)
        chosen = jnp.where(iota[...] == line, jnp.bfloat16(1), jnp.bfloat16(0))
        return jnp.dot(chosen, rows_of, preferred_element_type=jnp.float32)

    def contract(tile, count):
        pieces = []
        for t in range(2 * count):
            at = before + (2 * tile + t) * PITCH
            pieces.append(placed[pl.ds(at, GROUP), :].astype(jnp.bfloat16))
        both = jnp.concatenate(pieces, axis=1)
        kern = m2l_ref[:, pl.ds(pl.multiple_of(tile * 256, 256), 256 * count)]
        return lax.dot_general(both, kern, (((1,), (1,)), ((), ())), preferred_element_type=jnp.float32)

    out_ref[...] = jnp.zeros_like(out_ref)

    @pl.when(step < last)
    def _():
        def body(it, carry):
            cell = UNROLL * it
            mine = lax.rem(it, 2) * UNROLL
            other = UNROLL - mine
            part = contract(cell, UNROLL)
            olds = [held[other + u] for u in range(UNROLL)]
            results = []
            for u in range(UNROLL):
                back = jnp.where(it == 0, GROUP - UNROLL + u, cell - UNROLL + u)
                results.append((back, pick(back, olds[u])))
            collect([cell + u for u in range(UNROLL)], [mine + u for u in range(UNROLL)])
            for back, result in results:
                placed[pl.ds(now + back, PAIRS, stride=PITCH), :] = result
            out_ref[...] += part
            return carry
        lax.fori_loop(0, GROUP // UNROLL, body, 0)
        mine = (GROUP // UNROLL - 1) % 2 * UNROLL
        for u in range(UNROLL):
            back = GROUP - UNROLL + u
            placed[pl.ds(now + back, PAIRS, stride=PITCH), :] = pick(back, held[mine + u])

    @pl.when(step == last)
    def _():
        def body(it, carry):
            out_ref[...] += contract(it * UNROLL, UNROLL)
            return carry
        lax.fori_loop(0, GROUP // UNROLL, body, 0)


def translate(own, ghost, sources, offsets, m2l_kernels):
    leaves, inter = sources.shape
    ghosts = ghost.shape[0]
    rows = leaves + 2 * ghosts
    remote = sources - leaves
    row = jnp.where(remote < 0, sources, leaves + lax.shift_right_arithmetic(remote, 1) + (remote & 1) * ghosts)
    row = row + (offsets & 1) * rows
    row = row + 8 - jnp.arange(inter, dtype=jnp.int32)[None, :] % 8
    row = jnp.pad(row, ((0, 0), (0, SLOTS - inter))).reshape(-1)
    pair = jnp.pad((offsets >> 1).astype(jnp.float32), ((0, 0), (0, 256 - inter)), constant_values=-1.0)
    steps = leaves // GROUP
    return pl.pallas_call(
        functools.partial(translate_kernel, leaves, inter),
        grid=(steps + 1,),
        in_specs=[
            pl.BlockSpec((GROUP * SLOTS,), lambda i: (jnp.minimum(i, steps - 1),), memory_space=pltpu.SMEM),
            pl.BlockSpec((GROUP, 256), lambda i: (jnp.minimum(i, steps - 1), 0)),
            pl.BlockSpec(own.shape, lambda i: (0, 0)),
            pl.BlockSpec(ghost.shape, lambda i: (0, 0)),
            pl.BlockSpec(memory_space=pl.ANY),
        ],
        out_specs=pl.BlockSpec((GROUP, 64), lambda i: (jnp.maximum(i - 1, 0), 0)),
        out_shape=jax.ShapeDtypeStruct((leaves, 64), jnp.float32),
        scratch_shapes=[
            pltpu.VMEM((2 * rows + 16, 128), jnp.float32),
            pltpu.VMEM((PAIRS, 256), jnp.bfloat16),
            pltpu.VMEM((2 * UNROLL, 256, 128), jnp.bfloat16),
            pltpu.VMEM((2 * PAIRS * PITCH, 128), jnp.float32),
            pltpu.VMEM((RANK, PAIRS * 128), jnp.bfloat16),
            pltpu.SemaphoreType.DMA,
        ],
        compiler_params=params(),
    )(row, pair, own, ghost, m2l_kernels)


def evaluate_kernel(merged_ref, bodies_ref, leaf_ref, local_ref, expand_ref, out_ref, bodies, nodes0, nodes1, nodes2, nodes, result):
    step = pl.program_id(0)
    leaves = local_ref.shape[0]
    parts = (nodes0, nodes1, nodes2)

    @pl.when(step == 0)
    def _():
        full = lax.dot_general(
            expand_ref[...],
            local_ref[...],
            (((1,), (1,)), ((), ())),
            precision=lax.Precision.HIGHEST,
            preferred_element_type=jnp.float32,
        )
        for scratch, part in zip(parts, split_three(full)):
            scratch[...] = part

    @pl.when(step < SWAPS)
    def _():
        for dim in range(3):
            bodies[dim] = merged_ref[dim].T

    @pl.when(step >= SWAPS)
    def _():
        for dim in range(3):
            bodies[dim] = bodies_ref[dim].T

    onehot = lax.broadcasted_iota(jnp.int32, (leaves, REGION), 0) == leaf_ref[...]
    onehot = jnp.where(onehot, 1.0, 0.0).astype(jnp.bfloat16)
    total = jnp.dot(nodes0[...], onehot, preferred_element_type=jnp.float32)
    total += jnp.dot(nodes1[...], onehot, preferred_element_type=jnp.float32)
    total += jnp.dot(nodes2[...], onehot, preferred_element_type=jnp.float32)
    nodes[...] = total

    def chunk(v, carry):
        at = pl.ds(pl.multiple_of(v * 16, 16), 16)
        wx, wy, wz = (node_weights(bodies[dim, at, :]) for dim in range(3))
        value = None
        for i in range(ORDER):
            middle = None
            for j in range(ORDER):
                inner = None
                for k in range(ORDER):
                    term = nodes[pl.ds((i * ORDER + j) * ORDER + k, 1), :] * wz[k]
                    inner = term if inner is None else inner + term
                inner = inner * wy[j]
                middle = inner if middle is None else middle + inner
            middle = middle * wx[i]
            value = middle if value is None else value + middle
        result[at, :] = value
        return carry

    lax.fori_loop(0, BLOCK // 16, chunk, 0)
    out_ref[...] = result[...].T


def on_device(
    coords,
    masses,
    swap_counts,
    leaf_of_block,
    let_send,
    inter_source,
    inter_offset,
    compress,
    m2l_kernels,
    expand,
):
    nodes_count = compress.shape[0]
    leaves = inter_source.shape[0]
    local_bodies = coords.shape[1]
    blocks = local_bodies // BLOCK
    regions = blocks // REGION
    peers, per_peer = let_send.shape[1:]
    bodies = jnp.concatenate([coords.reshape(3, blocks, BLOCK), masses.reshape(1, blocks, BLOCK)], axis=0)
    top_bit = lax.axis_size("space").bit_length() - 2
    got_outer = from_partner(bodies[:, 0:REGION], "space", top_bit)
    got_inner = from_partner(bodies[:, REGION : 2 * REGION], "space", 0)
    got_sub = from_partner(bodies[:, 2 * REGION : 3 * REGION], "sub", 0)
    block4 = (4, REGION, BLOCK)
    stayed = pl.pallas_call(
        moments_kernel,
        grid=(regions - SWAPS,),
        in_specs=[pl.BlockSpec(block4, lambda g: (0, g + SWAPS, 0))],
        out_specs=pl.BlockSpec((nodes_count, REGION), lambda g: (0, g)),
        out_shape=jax.ShapeDtypeStruct((nodes_count, (regions - SWAPS) * REGION), jnp.float32),
        scratch_shapes=weight_scratch(),
        compiler_params=params(),
        cost_estimate=pl.CostEstimate(flops=50_000_000, bytes_accessed=4_000_000, transcendentals=0),
    )(bodies)
    whole4 = pl.BlockSpec(block4, lambda g: (0, 0, 0))
    swapped, merged = pl.pallas_call(
        swapped_moments_kernel,
        grid=(SWAPS,),
        in_specs=[
            pl.BlockSpec(memory_space=pltpu.SMEM),
            pl.BlockSpec(block4, lambda g: (0, g, 0)),
            whole4,
            whole4,
            whole4,
        ],
        out_specs=[
            pl.BlockSpec((nodes_count, REGION), lambda g: (0, g)),
            pl.BlockSpec(block4, lambda g: (0, g, 0)),
        ],
        out_shape=[
            jax.ShapeDtypeStruct((nodes_count, SWAPS * REGION), jnp.float32),
            jax.ShapeDtypeStruct((4, SWAPS * REGION, BLOCK), jnp.float32),
        ],
        scratch_shapes=weight_scratch(),
        compiler_params=params(),
    )(swap_counts.reshape(SWAPS), bodies, got_outer, got_inner, got_sub)
    leaf_row = leaf_of_block.reshape(1, blocks)
    send = let_send.reshape(peers, per_peer) + 8 - (jnp.arange(per_peer, dtype=jnp.int32)[None, :] // 2) % 8
    compress_twice = jnp.concatenate([compress.T, compress.T], axis=0)
    vmem = pl.BlockSpec(memory_space=pltpu.VMEM)
    own, outgoing = pl.pallas_call(
        coefficients_kernel,
        in_specs=[pl.BlockSpec(memory_space=pltpu.SMEM), vmem, vmem, vmem, vmem],
        out_specs=[vmem, vmem],
        out_shape=[
            jax.ShapeDtypeStruct((leaves, 2 * RANK), jnp.float32),
            jax.ShapeDtypeStruct((peers * per_peer // 2, 2 * RANK), jnp.bfloat16),
        ],
        scratch_shapes=[pltpu.VMEM((leaves + 16, 2 * RANK), jnp.float32)],
        compiler_params=params(),
    )(send.reshape(-1), swapped, stayed, leaf_row, compress_twice)
    incoming = lax.all_to_all(
        outgoing.reshape(peers, per_peer // 2, 2 * RANK), ("space", "sub"), split_axis=0, concat_axis=0, tiled=True
    )
    local = translate(own, incoming.reshape(peers * per_peer // 2, 2 * RANK), inter_source, inter_offset, m2l_kernels)
    values = pl.pallas_call(
        evaluate_kernel,
        grid=(regions,),
        in_specs=[
            pl.BlockSpec(block4, lambda g: (0, jnp.minimum(g, SWAPS - 1), 0)),
            pl.BlockSpec(block4, lambda g: (0, jnp.maximum(g, SWAPS), 0)),
            pl.BlockSpec((1, REGION), lambda g: (0, g)),
            pl.BlockSpec((leaves, RANK), lambda g: (0, 0)),
            pl.BlockSpec((nodes_count, RANK), lambda g: (0, 0)),
        ],
        out_specs=pl.BlockSpec((REGION, BLOCK), lambda g: (g, 0)),
        out_shape=jax.ShapeDtypeStruct((blocks, BLOCK), jnp.float32),
        scratch_shapes=[
            pltpu.VMEM((3, BLOCK, REGION), jnp.float32),
            pltpu.VMEM((nodes_count, leaves), jnp.bfloat16),
            pltpu.VMEM((nodes_count, leaves), jnp.bfloat16),
            pltpu.VMEM((nodes_count, leaves), jnp.bfloat16),
            pltpu.VMEM((nodes_count, REGION), jnp.float32),
            pltpu.VMEM((BLOCK, REGION), jnp.float32),
        ],
        compiler_params=params(),
    )(merged, bodies, leaf_row, local, expand.T)
    return values.reshape(local_bodies)


def solution(mesh):
    return jax.shard_map(
        on_device,
        mesh=mesh,
        in_specs=(
            P(None, ("space", "sub")),
            P(("space", "sub")),
            P(("space", "sub"), None),
            P(("space", "sub")),
            P(("space", "sub"), None, None),
            P(("space", "sub"), None),
            P(("space", "sub"), None),
            P(),
            P(),
            P(),
        ),
        out_specs=P(("space", "sub")),
        check_vma=False,
    )
```

time: 737 us -> 196 us (0.27); the launches traced: 727 us -> 195 us
  local copies, waits for them, and re-layouts: 439 us -> 6.93 us
  Pallas kernels: 0 us -> 161 us
  other arithmetic: 149 us -> 3.88 us
  matrix products: 97 us -> 0 us
  waiting for transfers between devices: 25.6 us -> 9.89 us
    gather x11 -> x0, local copies, waits for them, and re-layouts: 305 us -> none  [the longest x10 288 us: translate_block(): gathered = table[sources]]
    pallas_call x0 -> x5, Pallas kernels: none -> 161 us  [the longest x1 115 us: translate(): pl.pallas_call(functools.partial(translate_kernel, leaves, inter), grid=(...]
    dot_general x15 -> x0, matrix products: 97 us -> none  [the longest x5 62.8 us: translate_block(): lax.dot_general(selector, gathered, (((2,), (1,)), ((0,), (0,))), preferr...]
    reduce_sum x2 -> x0, other arithmetic: 66 us -> none  [the longest x1 34.1 us: on_device(): values = jnp.sum(pair_plain * inner, axis=0)]
    convert_element_type x5 -> x0, local copies, waits for them, and re-layouts: 46.8 us -> none  [translate_block(): placed.astype(jnp.bfloat16).reshape(target_rows, offsets_count * rank)]
    mul x2 -> x0, local copies, waits for them, and re-layouts: 38.5 us -> none  [the longest x1 19.3 us: on_device(): weights[:, 0][:, None, :] * weights[:, 1][None, :, :]]
    all_to_all x1 -> x0, other arithmetic: 37.1 us -> none  [on_device(): lax.all_to_all(outgoing, ('space', 'sub'), split_axis=0, concat_axis=0, t...]
    mul x5 -> x0, other arithmetic: 24.2 us -> none  [the longest x1 16.4 us: on_device(): (weights[:, 0] * stacked[3][None, :])[:, None, :]]
  transfers between devices with their start and end apart: 4 -> 4, of which waited for: 1 -> 1; matrix products, arithmetic and copies ran while one was open for 4% -> 3% of each run, Pallas kernels for 0% -> 6%
where the time goes in v1:
time: 196 us; the launch traced here: 195 us
  Pallas kernels  161 us (82%)
  starting transfers between devices  13.7 us (7%)
  waiting for transfers between devices  9.89 us (5%)
  local copies, waits for them, and re-layouts  6.93 us (4%)
  other arithmetic  3.88 us (2%)
    pallas_call x1, Pallas kernels, translate(): pl.pallas_call(functools.partial(translate_kernel, leaves, inter), grid=(...  115 us
    pallas_call x1, Pallas kernels, on_device(): pl.pallas_call(evaluate_kernel, grid=(regions,), in_specs=[pl.BlockSpec(b...  18.4 us
    pallas_call x1, Pallas kernels, on_device(): pl.pallas_call(moments_kernel, grid=(regions - SWAPS,), in_specs=[pl.Bloc...  11.2 us
    all_to_all x1, waiting for transfers between devices, on_device(): lax.all_to_all(outgoing.reshape(peers, per_peer // 2, 2 * RANK), ('space'...  9.88 us
    pallas_call x1, Pallas kernels, on_device(): pl.pallas_call(coefficients_kernel, in_specs=[pl.BlockSpec(memory_space=p...  8.32 us
    pallas_call x1, Pallas kernels, on_device(): pl.pallas_call(swapped_moments_kernel, grid=(SWAPS,), in_specs=[pl.BlockS...  7.95 us
    ppermute x3, starting transfers between devices, from_partner(): return lax.ppermute(block, axis, route)  6.87 us
    all_to_all x1, starting transfers between devices, on_device(): lax.all_to_all(outgoing.reshape(peers, per_peer // 2, 2 * RANK), ('space'...  6.79 us
  transfers between devices with their start and end apart: 4, of which 1 were waited for; matrix products, arithmetic and copies ran while one was open for 3% of the time, Pallas kernels for 6%

profile of v1, /device:TPU:1, one launch (start us, length us, event | category | flops | bytes accessed | tf_op | source)
XLA Modules:
  0.0 195.4 jit_solution(1105874411363073338)
XLA Ops:
  0.0 1.8 copy.29
  1.8 0.0 copy-start.9
  1.8 0.8 fusion.2
  2.6 4.4 %collective-permute-start = (f32[4,128,128]{2,1,0:T(8,128)}, f32[4,128,128]{2,1,0:T(8,128)S(1)}, u32[]{:S(2)}, u32[]{:S(2)}) collective-permute-start(f32[4,128,128]{2,1,0:T(8,128)} %get-tuple-element.14), channel_id=1, source_target_pairs={{0,64},{64,0},{8,72},{72,8},{16,80},{80,16},{24,88},{88,24},{32,96... | collective-permute-start | bytes 786440 | tf_op jit(solution)/shard_map/ppermute | solution.py:34
  7.1 1.2 collective-permute-start.1
  8.3 1.2 collective-permute-start.2
  9.5 0.1 copy.24
  9.6 0.1 add.66
  9.7 0.1 sub.33
  9.8 0.6 sub.34.send_ref
  10.4 1.5 pad_maximum_fusion.bodies_ref
  11.9 11.2 %shard_map.101.stayed_ref = f32[216,640]{1,0:T(8,128)} custom-call(f32[4,1024,128]{2,1,0:T(8,128)} %pad_maximum_fusion.bodies_ref), custom_call_target="tpu_custom_call" | custom-call | flops 50000000 | bytes 4000000 | tf_op jit(solution)/shard_map/pallas_call | solution.py:365
  23.1 0.7 pad_maximum_fusion.1.compress_ref
  23.8 0.0 collective-permute-done.got0_ref
  23.8 0.0 collective-permute-done.1.got1_ref
  23.8 0.7 copy-done.4
  24.5 0.1 copy-done.5
  24.5 0.1 copy-done.6
  24.6 8.0 %shard_map.100 = (f32[216,384]{1,0:T(8,128)}, f32[4,384,128]{2,1,0:T(8,128)}) custom-call(s32[3]{0:T(128)} %bitcast.23, f32[4,1024,128]{2,1,0:T(8,128)} %pad_maximum_fusion.bodies_ref, f32[4,128,128]{2,1,0:T(8,128)} %copy-done.4, f32[4,128,128]{2,1,0:T(8,128)} %copy-done.5, f32[4,128,128]{2,1,0:T(8,128)} %copy-done.6), custom_call_target="tpu_custom_call" | custom-call | tf_op jit(solution)/shard_map/pallas_call | solution.py:376
  32.6 8.3 %shard_map.102 = (f32[640,128]{1,0:T(8,128)}, bf16[2048,128]{1,0:T(8,128)(2,1)}) custom-call(s32[4096]{0:T(1024)} %sub.34.send_ref, f32[216,384]{1,0:T(8,128)} %get-tuple-element.10.swapped_ref, f32[216,640]{1,0:T(8,128)} %shard_map.101.stayed_ref, s32[1,1024]{1,0:T(1,128)} %bitcast.21, f32[128,216]{1,0:T(8,128)} %pad_maximum_fusion.1.compress_ref), custom_call_target="tpu_custom_call" | custom-call | tf_op jit(solution)/shard_map/pallas_call | solution.py:401
  40.9 6.8 %all-to-all-start = ((bf16[128,16,128]{2,1,0:T(8,128)(2,1)}), bf16[128,16,128]{2,1,0:T(8,128)(2,1)S(1)}, u32[]{:S(2)}, u32[]{:S(2)}) async-start(bf16[128,16,128]{2,1,0:T(8,128)(2,1)} %bitcast.18), calls=%async_computation | async-start | bytes 1048576 | tf_op jit(solution)/shard_map/all_to_all | solution.py:412
  47.7 0.2 broadcast_shift-right-arithmetic_fusion
  48.0 0.2 copy.23
  48.3 0.0 copy-start.8
  48.3 0.2 copy.26
  48.6 1.1 reshape.103.src_ref
  49.7 0.7 copy.25
  50.4 0.9 pad.9.off_ref
  51.3 9.9 %all-to-all-done = bf16[128,16,128]{2,1,0:T(8,128)(2,1)S(1)} async-done(((bf16[128,16,128]{2,1,0:T(8,128)(2,1)}), bf16[128,16,128]{2,1,0:T(8,128)(2,1)S(1)}, u32[]{:S(2)}, u32[]{:S(2)}) %all-to-all-start) | async-done | bytes 524320 | tf_op jit(solution)/shard_map/all_to_all | solution.py:412
  61.2 0.8 copy-done
  62.0 115.0 %shard_map.103.local_ref = f32[640,64]{1,0:T(8,128)} custom-call(s32[122880]{0:T(1024)} %reshape.103.src_ref, f32[640,256]{1,0:T(8,128)} %pad.9.off_ref, f32[640,128]{1,0:T(8,128)} %get-tuple-element.11.own_ref, bf16[2048,128]{1,0:T(8,128)(2,1)} %bitcast.15, bf16[64,20224]{1,0:T(8,128)(2,1)} %kernels_ref.1), custom_call_target="tpu_custom_call" | custom-call | tf_op jit(solution)/shard_map/pallas_call | solution.py:261
  177.0 18.4 %shard_map.104 = f32[1024,128]{1,0:T(8,128)} custom-call(f32[4,384,128]{2,1,0:T(8,128)} %get-tuple-element.9.merged_ref, f32[4,1024,128]{2,1,0:T(8,128)} %pad_maximum_fusion.bodies_ref, s32[1,1024]{1,0:T(1,128)} %bitcast.22, f32[640,64]{1,0:T(8,128)} %shard_map.103.local_ref, f32[216,64]{1,0:T(8,128)} %bitcast.19), custom_call_target="tpu_custom_call" | custom-call | tf_op jit(solution)/shard_map/pallas_call | solution.py:416
  (21 shorter events, 0.1 us)
Async XLA Ops:
  0.0 1.8 copy-start.1
  1.8 7.8 %copy-start.9 = (s32[1,128,32]{1,2,0:T(8,128)S(1)}, s32[1,128,32]{1,2,0:T(8,128)}, u32[]{:S(2)}) copy-start(s32[1,128,32]{1,2,0:T(8,128)} %param.14) | copy-start | bytes 49156
  2.6 21.1 %collective-permute-start = (f32[4,128,128]{2,1,0:T(8,128)}, f32[4,128,128]{2,1,0:T(8,128)S(1)}, u32[]{:S(2)}, u32[]{:S(2)}) collective-permute-start(f32[4,128,128]{2,1,0:T(8,128)} %get-tuple-element.14), channel_id=1, source_target_pairs={{0,64},{64,0},{8,72},{72,8},{16,80},{80,16},{24,88},{88,24},{32,96... | collective-permute-start | bytes 786440 | tf_op jit(solution)/shard_map/ppermute | solution.py:34
  7.1 16.7 %collective-permute-start.1 = (f32[4,128,128]{2,1,0:T(8,128)}, f32[4,128,128]{2,1,0:T(8,128)S(1)}, u32[]{:S(2)}, u32[]{:S(2)}) collective-permute-start(f32[4,128,128]{2,1,0:T(8,128)} %get-tuple-element.15), channel_id=1, source_target_pairs={{0,8},{8,0},{16,24},{24,16},{32,40},{40,32},{48,56},{56,48},{64,72... | collective-permute-start | bytes 786440 | tf_op jit(solution)/shard_map/ppermute | solution.py:34
  8.3 15.5 %collective-permute-start.2 = (f32[4,128,128]{2,1,0:T(8,128)S(1)}, f32[4,128,128]{2,1,0:T(8,128)S(1)}, u32[]{:S(2)}, u32[]{:S(2)}) collective-permute-start(f32[4,128,128]{2,1,0:T(8,128)S(1)} %get-tuple-element.13), channel_id=1, source_target_pairs={{0,1},{1,0},{2,3},{3,2},{4,5},{5,4},{6,7},{7,6},{8,9},{9,8},{10,11... | collective-permute-start | bytes 786440 | tf_op jit(solution)/shard_map/ppermute | solution.py:34
  11.9 11.2 %copy-start.7 = (f32[216,64]{0,1:T(8,128)S(1)}, f32[216,64]{0,1:T(8,128)}, u32[]{:S(2)}) copy-start(f32[216,64]{0,1:T(8,128)} %param.17) | copy-start | bytes 165892
  23.8 0.7 copy-start.4
  23.8 0.8 copy-start.5
  23.8 0.8 copy-start.6
  24.6 23.1 %copy-start.2 = (s32[640,189]{0,1:T(8,128)S(1)}, s32[640,189]{0,1:T(8,128)}, u32[]{:S(2)}) copy-start(s32[640,189]{0,1:T(8,128)} %param.16) | copy-start | bytes 1451524
  24.6 23.1 %copy-start.3 = (s32[640,189]{0,1:T(8,128)S(1)}, s32[640,189]{0,1:T(8,128)}, u32[]{:S(2)}) copy-start(s32[640,189]{0,1:T(8,128)} %param.15) | copy-start | bytes 1451524
  40.9 20.3 %all-to-all-start = ((bf16[128,16,128]{2,1,0:T(8,128)(2,1)}), bf16[128,16,128]{2,1,0:T(8,128)(2,1)S(1)}, u32[]{:S(2)}, u32[]{:S(2)}) async-start(bf16[128,16,128]{2,1,0:T(8,128)(2,1)} %bitcast.18), calls=%async_computation | async-start | bytes 1048576 | tf_op jit(solution)/shard_map/all_to_all | solution.py:412
  48.3 1.4 copy-start.8
  61.2 0.8 copy-start

commit v2 on v1

--- a/solution.py
+++ b/solution.py
@@ -17,7 +17,7 @@
 SLOTS = 192
 PAIRS = 160
 PITCH = 81
-UNROLL = 4
+UNROLL = 8
 
 
 def params(**more):
@@ -34,63 +34,70 @@
     return lax.ppermute(block, axis, route)
 
 
-def node_weights(points):
+def chebyshev(points):
     twice = 2.0 * points
-    polys = [None, points, twice * points - 1.0]
-    for _ in range(3):
+    polys = [points, twice * points - 1.0]
+    for _ in range(ORDER - 3):
         polys.append(twice * polys[-1] - polys[-2])
-    weights = [None] * ORDER
-    for j in range(ORDER // 2):
-        c = [np.float32(np.cos(k * (2 * j + 1) * np.pi / (2 * ORDER)) / 3.0) for k in range(ORDER)]
-        even = np.float32(1.0 / ORDER) + c[2] * polys[2] + c[4] * polys[4]
-        odd = c[1] * polys[1] + c[3] * polys[3] + c[5] * polys[5]
-        weights[j] = even + odd
-        weights[ORDER - 1 - j] = even - odd
-    return weights
-
-
-def split_three(values):
+    return polys
+
+
+def node_basis():
+    single = np.zeros((ORDER, ORDER))
+    for j in range(ORDER):
+        for k in range(ORDER):
+            single[j, k] = np.cos(k * (2 * j + 1) * np.pi / (2 * ORDER)) * (1.0 if k == 0 else 2.0) / ORDER
+    return np.kron(np.kron(single, single), single).astype(np.float32)
+
+
+def split_two(values):
     first = values.astype(jnp.bfloat16)
-    rest = values - first.astype(jnp.float32)
-    second = rest.astype(jnp.bfloat16)
-    third = (rest - second.astype(jnp.float32)).astype(jnp.bfloat16)
-    return first, second, third
-
-
-def gather_moments(bodies, out_ref, wx, wy, wz):
+    return first, (values - first.astype(jnp.float32)).astype(jnp.bfloat16)
+
+
+def gather_moments(bodies, out_ref, turned_ref, px, py, pz, partial):
     mass = bodies[3].T
-    for j, weight in enumerate(node_weights(bodies[0].T)):
-        wx[j] = weight * mass
-    for scratch, dim in ((wy, 1), (wz, 2)):
-        for j, weight in enumerate(node_weights(bodies[dim].T)):
-            scratch[j] = weight
+    px[0] = mass
+    for dim, scratch in enumerate((px, py, pz)):
+        points = bodies[dim].T
+        turned_ref[dim] = points
+        for k, poly in enumerate(chebyshev(points)):
+            scratch[k + 1] = poly * mass if dim == 0 else poly
 
     def along(i, carry):
         def chunk(v, sums):
             at = pl.ds(pl.multiple_of(v * 8, 8), 8)
-            left = wx[i, at, :]
-            inner = [wz[k, at, :] for k in range(ORDER)]
+            left = px[i, at, :]
+            inner = [pz[k, at, :] for k in range(1, ORDER)]
             new = []
             for j in range(ORDER):
-                pair = left * wy[j, at, :]
-                for k in range(ORDER):
-                    new.append(sums[j * ORDER + k] + pair * inner[k])
+                pair = left if j == 0 else left * py[j, at, :]
+                new.append(sums[j * ORDER] + pair)
+                for k in range(1, ORDER):
+                    new.append(sums[j * ORDER + k] + pair * inner[k - 1])
             return tuple(new)
 
         zero = jnp.zeros((8, REGION), jnp.float32)
         sums = lax.fori_loop(0, BLOCK // 8, chunk, (zero,) * (ORDER * ORDER), unroll=4)
         for n in range(ORDER * ORDER):
-            out_ref[pl.ds(i * ORDER * ORDER + n, 1), :] = jnp.sum(sums[n], axis=0, keepdims=True)
+            partial[pl.ds(pl.multiple_of((i * ORDER * ORDER + n) * 8, 8), 8), :] = sums[n]
         return carry
 
     lax.fori_loop(0, ORDER, along, 0)
-
-
-def moments_kernel(bodies_ref, out_ref, wx, wy, wz):
-    gather_moments(bodies_ref, out_ref, wx, wy, wz)
-
-
-def swapped_moments_kernel(counts_ref, bodies_ref, got0_ref, got1_ref, got2_ref, out_ref, merged_ref, wx, wy, wz):
+    count = out_ref.shape[0]
+    total = partial[pl.ds(0, count, stride=8), :]
+    for s in range(1, 8):
+        total += partial[pl.ds(s, count, stride=8), :]
+    out_ref[...] = total
+
+
+def moments_kernel(bodies_ref, out_ref, turned_ref, px, py, pz, partial):
+    gather_moments(bodies_ref, out_ref, turned_ref, px, py, pz, partial)
+
+
+def swapped_moments_kernel(
+    counts_ref, bodies_ref, got0_ref, got1_ref, got2_ref, out_ref, turned_ref, merged, px, py, pz, partial
+):
     column = lax.broadcasted_iota(jnp.int32, (REGION, BLOCK), 0) * BLOCK + lax.broadcasted_iota(
         jnp.int32, (REGION, BLOCK), 1
     )
@@ -100,13 +107,15 @@
         def _():
             keep = column < counts_ref[rnd]
             for dim in range(4):
-                merged_ref[dim] = jnp.where(keep, got[dim], bodies_ref[dim])
-
-    gather_moments(merged_ref, out_ref, wx, wy, wz)
-
-
-def weight_scratch():
-    return [pltpu.VMEM((ORDER, BLOCK, REGION), jnp.float32) for _ in range(3)]
+                merged[dim] = jnp.where(keep, got[dim], bodies_ref[dim])
+
+    gather_moments(merged, out_ref, turned_ref, px, py, pz, partial)
+
+
+def moment_scratch(nodes_count):
+    return [pltpu.VMEM((ORDER, BLOCK, REGION), jnp.float32) for _ in range(3)] + [
+        pltpu.VMEM((8 * nodes_count, REGION), jnp.float32)
+    ]
 
 
 def coefficients_kernel(send_ref, swapped_ref, stayed_ref, leaf_ref, compress_ref, own_ref, out_ref, padded):
@@ -122,10 +131,10 @@
         moved = jnp.dot(
             compress_ref[...], sums[...], precision=lax.Precision.HIGHEST, preferred_element_type=jnp.float32
         )
-        for part in split_three(moved):
-            total += lax.dot_general(onehot, part, (((1,), (1,)), ((), ())), preferred_element_type=jnp.float32)
+        both = jnp.concatenate(split_two(moved), axis=0)
+        total += lax.dot_general(onehot, both, (((1,), (1,)), ((), ())), preferred_element_type=jnp.float32)
         at += count
-    own = total.astype(jnp.bfloat16).astype(jnp.float32)
+    own = (total + pltpu.roll(total, RANK, 1)).astype(jnp.bfloat16).astype(jnp.float32)
     own_ref[...] = own
     padded[pl.ds(0, 8), :] = jnp.zeros((8, 2 * RANK), jnp.float32)
     padded[pl.ds(8, leaves), :] = own
@@ -220,24 +229,21 @@
     def _():
         def body(it, carry):
             cell = UNROLL * it
-            mine = lax.rem(it, 2) * UNROLL
-            other = UNROLL - mine
             part = contract(cell, UNROLL)
-            olds = [held[other + u] for u in range(UNROLL)]
+            olds = [held[u] for u in range(UNROLL)]
             results = []
             for u in range(UNROLL):
-                back = jnp.where(it == 0, GROUP - UNROLL + u, cell - UNROLL + u)
+                back = jnp.where(it == 0, GROUP - UNROLL, cell - UNROLL) + u
                 results.append((back, pick(back, olds[u])))
-            collect([cell + u for u in range(UNROLL)], [mine + u for u in range(UNROLL)])
+            collect([cell + u for u in range(UNROLL)], list(range(UNROLL)))
             for back, result in results:
                 placed[pl.ds(now + back, PAIRS, stride=PITCH), :] = result
             out_ref[...] += part
             return carry
         lax.fori_loop(0, GROUP // UNROLL, body, 0)
-        mine = (GROUP // UNROLL - 1) % 2 * UNROLL
         for u in range(UNROLL):
             back = GROUP - UNROLL + u
-            placed[pl.ds(now + back, PAIRS, stride=PITCH), :] = pick(back, held[mine + u])
+            placed[pl.ds(now + back, PAIRS, stride=PITCH), :] = pick(back, held[u])
 
     @pl.when(step == last)
     def _():
@@ -273,7 +279,7 @@
         scratch_shapes=[
             pltpu.VMEM((2 * rows + 16, 128), jnp.float32),
             pltpu.VMEM((PAIRS, 256), jnp.bfloat16),
-            pltpu.VMEM((2 * UNROLL, 256, 128), jnp.bfloat16),
+            pltpu.VMEM((UNROLL, 256, 128), jnp.bfloat16),
             pltpu.VMEM((2 * PAIRS * PITCH, 128), jnp.float32),
             pltpu.VMEM((RANK, PAIRS * 128), jnp.bfloat16),
             pltpu.SemaphoreType.DMA,
@@ -282,10 +288,10 @@
     )(row, pair, own, ghost, m2l_kernels)
 
 
-def evaluate_kernel(merged_ref, bodies_ref, leaf_ref, local_ref, expand_ref, out_ref, bodies, nodes0, nodes1, nodes2, nodes, result):
+def evaluate_kernel(swapped_ref, stayed_ref, leaf_ref, local_ref, expand_ref, out_ref, bodies, nodes, result):
     step = pl.program_id(0)
     leaves = local_ref.shape[0]
-    parts = (nodes0, nodes1, nodes2)
+    count = expand_ref.shape[0]
 
     @pl.when(step == 0)
     def _():
@@ -296,41 +302,35 @@
             precision=lax.Precision.HIGHEST,
             preferred_element_type=jnp.float32,
         )
-        for scratch, part in zip(parts, split_three(full)):
-            scratch[...] = part
+        parts = jnp.concatenate(split_two(full), axis=0)
+        for region in range(nodes.shape[0]):
+            ids = leaf_ref[:, pl.ds(region * REGION, REGION)]
+            onehot = lax.broadcasted_iota(jnp.int32, (leaves, REGION), 0) == ids
+            onehot = jnp.where(onehot, 1.0, 0.0).astype(jnp.bfloat16)
+            picked = jnp.dot(parts, onehot, preferred_element_type=jnp.float32)
+            nodes[region] = picked[:count] + picked[count:]
 
     @pl.when(step < SWAPS)
     def _():
-        for dim in range(3):
-            bodies[dim] = merged_ref[dim].T
+        bodies[...] = swapped_ref[...]
 
     @pl.when(step >= SWAPS)
     def _():
-        for dim in range(3):
-            bodies[dim] = bodies_ref[dim].T
-
-    onehot = lax.broadcasted_iota(jnp.int32, (leaves, REGION), 0) == leaf_ref[...]
-    onehot = jnp.where(onehot, 1.0, 0.0).astype(jnp.bfloat16)
-    total = jnp.dot(nodes0[...], onehot, preferred_element_type=jnp.float32)
-    total += jnp.dot(nodes1[...], onehot, preferred_element_type=jnp.float32)
-    total += jnp.dot(nodes2[...], onehot, preferred_element_type=jnp.float32)
-    nodes[...] = total
+        bodies[...] = stayed_ref[...]
 
     def chunk(v, carry):
         at = pl.ds(pl.multiple_of(v * 16, 16), 16)
-        wx, wy, wz = (node_weights(bodies[dim, at, :]) for dim in range(3))
+        px, py, pz = (chebyshev(bodies[dim, at, :]) for dim in range(3))
         value = None
         for i in range(ORDER):
             middle = None
             for j in range(ORDER):
-                inner = None
-                for k in range(ORDER):
-                    term = nodes[pl.ds((i * ORDER + j) * ORDER + k, 1), :] * wz[k]
-                    inner = term if inner is None else inner + term
-                inner = inner * wy[j]
-                middle = inner if middle is None else middle + inner
-            middle = middle * wx[i]
-            value = middle if value is None else value + middle
+                first = (i * ORDER + j) * ORDER
+                inner = nodes[step, pl.ds(first + 1, 1), :] * pz[0] + nodes[step, pl.ds(first, 1), :]
+                for k in range(2, ORDER):
+                    inner += nodes[step, pl.ds(first + k, 1), :] * pz[k - 1]
+                middle = inner if j == 0 else middle + inner * py[j - 1]
+            value = middle if i == 0 else value + middle * px[i - 1]
         result[at, :] = value
         return carry
 
@@ -362,18 +362,24 @@
     got_inner = from_partner(bodies[:, REGION : 2 * REGION], "space", 0)
     got_sub = from_partner(bodies[:, 2 * REGION : 3 * REGION], "sub", 0)
     block4 = (4, REGION, BLOCK)
-    stayed = pl.pallas_call(
+    sums_spec = pl.BlockSpec((nodes_count, REGION), lambda g: (0, g))
+    turned_spec = pl.BlockSpec((3, BLOCK, REGION), lambda g: (0, 0, g))
+    stays = regions - SWAPS
+    stayed, stayed_turned = pl.pallas_call(
         moments_kernel,
-        grid=(regions - SWAPS,),
+        grid=(stays,),
         in_specs=[pl.BlockSpec(block4, lambda g: (0, g + SWAPS, 0))],
-        out_specs=pl.BlockSpec((nodes_count, REGION), lambda g: (0, g)),
-        out_shape=jax.ShapeDtypeStruct((nodes_count, (regions - SWAPS) * REGION), jnp.float32),
-        scratch_shapes=weight_scratch(),
+        out_specs=[sums_spec, turned_spec],
+        out_shape=[
+            jax.ShapeDtypeStruct((nodes_count, stays * REGION), jnp.float32),
+            jax.ShapeDtypeStruct((3, BLOCK, stays * REGION), jnp.float32),
+        ],
+        scratch_shapes=moment_scratch(nodes_count),
         compiler_params=params(),
         cost_estimate=pl.CostEstimate(flops=50_000_000, bytes_accessed=4_000_000, transcendentals=0),
     )(bodies)
     whole4 = pl.BlockSpec(block4, lambda g: (0, 0, 0))
-    swapped, merged = pl.pallas_call(
+    swapped, swapped_turned = pl.pallas_call(
         swapped_moments_kernel,
         grid=(SWAPS,),
         in_specs=[
@@ -383,20 +389,20 @@
             whole4,
             whole4,
         ],
-        out_specs=[
-            pl.BlockSpec((nodes_count, REGION), lambda g: (0, g)),
-            pl.BlockSpec(block4, lambda g: (0, g, 0)),
-        ],
+        out_specs=[sums_spec, turned_spec],
         out_shape=[
             jax.ShapeDtypeStruct((nodes_count, SWAPS * REGION), jnp.float32),
-            jax.ShapeDtypeStruct((4, SWAPS * REGION, BLOCK), jnp.float32),
-        ],
-        scratch_shapes=weight_scratch(),
+            jax.ShapeDtypeStruct((3, BLOCK, SWAPS * REGION), jnp.float32),
+        ],
+        scratch_shapes=[pltpu.VMEM(block4, jnp.float32)] + moment_scratch(nodes_count),
         compiler_params=params(),
     )(swap_counts.reshape(SWAPS), bodies, got_outer, got_inner, got_sub)
+    basis = node_basis()
+    exact = functools.partial(jnp.dot, precision=lax.Precision.HIGHEST, preferred_element_type=jnp.float32)
+    compress_polys = exact(compress.T, basis)
+    expand_polys = exact(basis.T, expand.T)
     leaf_row = leaf_of_block.reshape(1, blocks)
     send = let_send.reshape(peers, per_peer) + 8 - (jnp.arange(per_peer, dtype=jnp.int32)[None, :] // 2) % 8
-    compress_twice = jnp.concatenate([compress.T, compress.T], axis=0)
     vmem = pl.BlockSpec(memory_space=pltpu.VMEM)
     own, outgoing = pl.pallas_call(
         coefficients_kernel,
@@ -408,7 +414,7 @@
         ],
         scratch_shapes=[pltpu.VMEM((leaves + 16, 2 * RANK), jnp.float32)],
         compiler_params=params(),
-    )(send.reshape(-1), swapped, stayed, leaf_row, compress_twice)
+    )(send.reshape(-1), swapped, stayed, leaf_row, compress_polys)
     incoming = lax.all_to_all(
         outgoing.reshape(peers, per_peer // 2, 2 * RANK), ("space", "sub"), split_axis=0, concat_axis=0, tiled=True
     )
@@ -417,9 +423,9 @@
         evaluate_kernel,
         grid=(regions,),
         in_specs=[
-            pl.BlockSpec(block4, lambda g: (0, jnp.minimum(g, SWAPS - 1), 0)),
-            pl.BlockSpec(block4, lambda g: (0, jnp.maximum(g, SWAPS), 0)),
-            pl.BlockSpec((1, REGION), lambda g: (0, g)),
+            pl.BlockSpec((3, BLOCK, REGION), lambda g: (0, 0, jnp.minimum(g, SWAPS - 1))),
+            pl.BlockSpec((3, BLOCK, REGION), lambda g: (0, 0, jnp.maximum(g - SWAPS, 0))),
+            pl.BlockSpec((1, blocks), lambda g: (0, 0)),
             pl.BlockSpec((leaves, RANK), lambda g: (0, 0)),
             pl.BlockSpec((nodes_count, RANK), lambda g: (0, 0)),
         ],
@@ -427,14 +433,11 @@
         out_shape=jax.ShapeDtypeStruct((blocks, BLOCK), jnp.float32),
         scratch_shapes=[
             pltpu.VMEM((3, BLOCK, REGION), jnp.float32),
-            pltpu.VMEM((nodes_count, leaves), jnp.bfloat16),
-            pltpu.VMEM((nodes_count, leaves), jnp.bfloat16),
-            pltpu.VMEM((nodes_count, leaves), jnp.bfloat16),
-            pltpu.VMEM((nodes_count, REGION), jnp.float32),
+            pltpu.VMEM((regions, nodes_count, REGION), jnp.float32),
             pltpu.VMEM((BLOCK, REGION), jnp.float32),
         ],
         compiler_params=params(),
-    )(merged, bodies, leaf_row, local, expand.T)
+    )(swapped_turned, stayed_turned, leaf_row, local, expand_polys)
     return values.reshape(local_bodies)
 
 

time: 196 us -> 175 us (0.89)
  Pallas kernels: 161 us -> 141 us
    pallas_call x1, Pallas kernels: 115 us -> 103 us  [translate(): pl.pallas_call(functools.partial(translate_kernel, leaves, inter), grid=(...]
    pallas_call x2, Pallas kernels: 29.6 us -> 23.5 us  [the longest x1 14.2 us: on_device(): pl.pallas_call(evaluate_kernel, grid=(regions,), in_specs=[pl.BlockSpec((...]
    unnamed x23 -> x26, local copies, waits for them, and re-layouts: 4.38 us -> 3.65 us
  transfers between devices with their start and end apart: 4 -> 4, of which waited for: 1 -> 1; matrix products, arithmetic and copies ran while one was open for 3% -> 4% of each run, Pallas kernels for 6% -> 5%
where the time goes in v2:
time: 175 us
  Pallas kernels  141 us (81%)
  starting transfers between devices  13.7 us (8%)
  waiting for transfers between devices  9.61 us (5%)
  local copies, waits for them, and re-layouts  6.23 us (4%)
  other arithmetic  2.42 us (1%)
  matrix products  1.86 us (1%)
    pallas_call x1, Pallas kernels, translate(): pl.pallas_call(functools.partial(translate_kernel, leaves, inter), grid=(...  103 us
    pallas_call x1, Pallas kernels, on_device(): pl.pallas_call(evaluate_kernel, grid=(regions,), in_specs=[pl.BlockSpec((...  14.2 us
    all_to_all x1, waiting for transfers between devices, on_device(): lax.all_to_all(outgoing.reshape(peers, per_peer // 2, 2 * RANK), ('space'...  9.6 us
    pallas_call x1, Pallas kernels, on_device(): pl.pallas_call(moments_kernel, grid=(stays,), in_specs=[pl.BlockSpec(bloc...  9.3 us
    pallas_call x1, Pallas kernels, on_device(): pl.pallas_call(coefficients_kernel, in_specs=[pl.BlockSpec(memory_space=p...  7.48 us
    ppermute x3, starting transfers between devices, from_partner(): return lax.ppermute(block, axis, route)  6.95 us
    all_to_all x1, starting transfers between devices, on_device(): lax.all_to_all(outgoing.reshape(peers, per_peer // 2, 2 * RANK), ('space'...  6.79 us
    pallas_call x1, Pallas kernels, on_device(): pl.pallas_call(swapped_moments_kernel, grid=(SWAPS,), in_specs=[pl.BlockS...  6.73 us
  transfers between devices with their start and end apart: 4, of which 1 were waited for; matrix products, arithmetic and copies ran while one was open for 4% of the time, Pallas kernels for 5%

profile of v2, /device:TPU:1, one launch (start us, length us, event | category | flops | bytes accessed | tf_op | source)
XLA Modules:
  0.0 175.1 jit_solution(2761772642135387110)
XLA Ops:
  0.0 1.8 %copy.32 = f32[1,3,1024,128]{3,2,1,0:T(8,128)S(1)} copy(f32[1,3,1024,128]{3,1,2,0:T(4,128)} %bitcast.18) | data formatting | bytes 3145728
  1.8 0.1 fusion.2
  1.8 4.5 %collective-permute-start = (f32[4,128,128]{2,1,0:T(8,128)S(1)}, f32[4,128,128]{2,1,0:T(8,128)S(1)}, u32[]{:S(2)}, u32[]{:S(2)}) collective-permute-start(f32[4,128,128]{2,1,0:T(8,128)S(1)} %get-tuple-element.18), channel_id=1, source_target_pairs={{0,64},{64,0},{8,72},{72,8},{16,80},{80,16},{24,88},{88,24},{32,96... | collective-permute-start | bytes 786440 | tf_op jit(solution)/shard_map/ppermute | solution.py:34
  6.3 1.2 collective-permute-start.1
  7.6 1.2 collective-permute-start.2
  8.8 1.5 pad_maximum_fusion.bodies_ref
  10.3 0.1 copy.26
  10.4 0.1 add.66
  10.5 0.1 sub.33
  10.6 0.6 sub.34.send_ref
  11.2 9.3 %shard_map.119 = (f32[216,640]{1,0:T(8,128)}, f32[3,128,640]{2,1,0:T(8,128)}) custom-call(f32[4,1024,128]{2,1,0:T(8,128)} %pad_maximum_fusion.bodies_ref), custom_call_target="tpu_custom_call" | custom-call | flops 50000000 | bytes 4000000 | tf_op jit(solution)/shard_map/pallas_call | solution.py:368
  20.5 0.9 convolution_bitcast_fusion.compress_ref
  21.4 0.0 collective-permute-done.got0_ref
  21.4 0.0 collective-permute-done.2.got2_ref
  21.4 0.7 copy-done.5
  22.1 0.1 copy-done.6
  22.2 0.1 copy-done.7
  22.2 6.7 %shard_map.118 = (f32[216,384]{1,0:T(8,128)}, f32[3,128,384]{2,1,0:T(8,128)}) custom-call(s32[3]{0:T(128)} %bitcast.25, f32[4,1024,128]{2,1,0:T(8,128)} %pad_maximum_fusion.bodies_ref, f32[4,128,128]{2,1,0:T(8,128)} %copy-done.5, f32[4,128,128]{2,1,0:T(8,128)} %copy-done.6, f32[4,128,128]{2,1,0:T(8,128)} %copy-done.7), custom_call_target="tpu_custom_call" | custom-call | tf_op jit(solution)/shard_map/pallas_call | solution.py:382
  29.0 7.5 %shard_map.120 = (f32[640,128]{1,0:T(8,128)}, bf16[2048,128]{1,0:T(8,128)(2,1)}) custom-call(s32[4096]{0:T(1024)} %sub.34.send_ref, f32[216,384]{1,0:T(8,128)} %get-tuple-element.13.swapped_ref, f32[216,640]{1,0:T(8,128)} %get-tuple-element.14.stayed_ref, s32[1,1024]{1,0:T(1,128)} %bitcast.23, f32[64,216]{1,0:T(8,128)} %convolution_bitcast_fusion.compress_ref), custom_call_target="tpu_custom_call" | custom-call | tf_op jit(solution)/shard_map/pallas_call | solution.py:407
  36.4 6.8 %all-to-all-start = ((bf16[128,16,128]{2,1,0:T(8,128)(2,1)}), bf16[128,16,128]{2,1,0:T(8,128)(2,1)S(1)}, u32[]{:S(2)}, u32[]{:S(2)}) async-start(bf16[128,16,128]{2,1,0:T(8,128)(2,1)} %bitcast.22), calls=%async_computation | async-start | bytes 1048576 | tf_op jit(solution)/shard_map/all_to_all | solution.py:418
  43.3 0.2 broadcast_shift-right-arithmetic_fusion
  43.5 0.2 copy.25
  43.8 0.2 copy.29
  44.0 0.0 copy-start.8
  44.1 0.0 copy-start.10
  44.1 1.1 reshape.103.src_ref
  45.3 0.9 pad.9.off_ref
  46.2 1.0 fusion.4.expand_ref
  47.1 9.6 %all-to-all-done = bf16[128,16,128]{2,1,0:T(8,128)(2,1)S(1)} async-done(((bf16[128,16,128]{2,1,0:T(8,128)(2,1)}), bf16[128,16,128]{2,1,0:T(8,128)(2,1)S(1)}, u32[]{:S(2)}, u32[]{:S(2)}) %all-to-all-start) | async-done | bytes 524320 | tf_op jit(solution)/shard_map/all_to_all | solution.py:418
  56.8 0.8 copy-done.1
  57.5 103.4 %shard_map.121.local_ref = f32[640,64]{1,0:T(8,128)} custom-call(s32[122880]{0:T(1024)} %reshape.103.src_ref, f32[640,256]{1,0:T(8,128)} %pad.9.off_ref, f32[640,128]{1,0:T(8,128)} %get-tuple-element.15.own_ref, bf16[2048,128]{1,0:T(8,128)(2,1)} %bitcast.19, bf16[64,20224]{1,0:T(8,128)(2,1)} %kernels_ref.1), custom_call_target="tpu_custom_call" | custom-call | tf_op jit(solution)/shard_map/pallas_call | solution.py:267
  160.9 14.2 %shard_map.122 = f32[1024,128]{1,0:T(8,128)} custom-call(f32[3,128,384]{2,1,0:T(8,128)} %get-tuple-element.11.swapped_ref, f32[3,128,640]{2,1,0:T(8,128)} %get-tuple-element.12.stayed_ref, s32[1,1024]{1,0:T(1,128)} %bitcast.24, f32[640,64]{1,0:T(8,128)} %shard_map.121.local_ref, f32[216,64]{1,0:T(8,128)} %fusion.4.expand_ref), custom_call_target="tpu_custom_call" | custom-call | tf_op jit(solution)/shard_map/pallas_call | solution.py:422
  (25 shorter events, 0.1 us)
Async XLA Ops:
  0.0 20.5 %copy-start = (f32[216,64]{0,1:T(8,128)S(1)}, f32[216,64]{0,1:T(8,128)}, u32[]{:S(2)}) copy-start(f32[216,64]{0,1:T(8,128)} %param.19) | copy-start | bytes 165892
  0.0 1.8 %copy-start.2 = (f32[131072]{0:T(1024)S(1)}, f32[131072]{0:T(1024)}, u32[]{:S(2)}) copy-start(f32[131072]{0:T(1024)} %param.13) | copy-start | bytes 1572868
  1.8 19.5 %collective-permute-start = (f32[4,128,128]{2,1,0:T(8,128)S(1)}, f32[4,128,128]{2,1,0:T(8,128)S(1)}, u32[]{:S(2)}, u32[]{:S(2)}) collective-permute-start(f32[4,128,128]{2,1,0:T(8,128)S(1)} %get-tuple-element.18), channel_id=1, source_target_pairs={{0,64},{64,0},{8,72},{72,8},{16,80},{80,16},{24,88},{88,24},{32,96... | collective-permute-start | bytes 786440 | tf_op jit(solution)/shard_map/ppermute | solution.py:34
  6.3 15.0 %collective-permute-start.1 = (f32[4,128,128]{2,1,0:T(8,128)S(1)}, f32[4,128,128]{2,1,0:T(8,128)S(1)}, u32[]{:S(2)}, u32[]{:S(2)}) collective-permute-start(f32[4,128,128]{2,1,0:T(8,128)S(1)} %get-tuple-element.19), channel_id=1, source_target_pairs={{0,8},{8,0},{16,24},{24,16},{32,40},{40,32},{48,56},{56,48},{64,72... | collective-permute-start | bytes 786440 | tf_op jit(solution)/shard_map/ppermute | solution.py:34
  7.6 2.7 %copy-start.11 = (s32[1,128,32]{1,2,0:T(8,128)S(1)}, s32[1,128,32]{1,2,0:T(8,128)}, u32[]{:S(2)}) copy-start(s32[1,128,32]{1,2,0:T(8,128)} %param.16) | copy-start | bytes 49156
  7.6 13.8 %collective-permute-start.2 = (f32[4,128,128]{2,1,0:T(8,128)S(1)}, f32[4,128,128]{2,1,0:T(8,128)S(1)}, u32[]{:S(2)}, u32[]{:S(2)}) collective-permute-start(f32[4,128,128]{2,1,0:T(8,128)S(1)} %get-tuple-element.17), channel_id=1, source_target_pairs={{0,1},{1,0},{2,3},{3,2},{4,5},{5,4},{6,7},{7,6},{8,9},{9,8},{10,11... | collective-permute-start | bytes 786440 | tf_op jit(solution)/shard_map/ppermute | solution.py:34
  10.3 10.2 %copy-start.9 = (f32[216,216]{1,0:T(8,128)S(1)}, f32[216,216]{1,0:T(8,128)}, u32[]{:S(2)}) copy-start(f32[216,216]{1,0:T(8,128)} %constant.58.clone) | copy-start | bytes 559876
  21.4 0.7 copy-start.5
  21.4 0.8 copy-start.6
  21.4 0.8 copy-start.7
  22.2 21.0 %copy-start.3 = (s32[640,189]{0,1:T(8,128)S(1)}, s32[640,189]{0,1:T(8,128)}, u32[]{:S(2)}) copy-start(s32[640,189]{0,1:T(8,128)} %param.18) | copy-start | bytes 1451524
  22.2 21.0 %copy-start.4 = (s32[640,189]{0,1:T(8,128)S(1)}, s32[640,189]{0,1:T(8,128)}, u32[]{:S(2)}) copy-start(s32[640,189]{0,1:T(8,128)} %param.17) | copy-start | bytes 1451524
  36.4 20.3 %all-to-all-start = ((bf16[128,16,128]{2,1,0:T(8,128)(2,1)}), bf16[128,16,128]{2,1,0:T(8,128)(2,1)S(1)}, u32[]{:S(2)}, u32[]{:S(2)}) async-start(bf16[128,16,128]{2,1,0:T(8,128)(2,1)} %bitcast.22), calls=%async_computation | async-start | bytes 1048576 | tf_op jit(solution)/shard_map/all_to_all | solution.py:418
  44.0 2.1 %copy-start.8 = (f32[216,216]{1,0:T(8,128)S(1)}, f32[216,216]{1,0:T(8,128)}, u32[]{:S(2)}) copy-start(f32[216,216]{1,0:T(8,128)} %constant.59.clone) | copy-start | bytes 559876
  44.1 2.1 %copy-start.10 = (f32[64,216]{1,0:T(8,128)S(1)}, f32[64,216]{1,0:T(8,128)}, u32[]{:S(2)}) copy-start(f32[64,216]{1,0:T(8,128)} %param.21) | copy-start | bytes 165892
  56.8 0.8 copy-start.1

commit v3 on v2

--- a/solution.py
+++ b/solution.py
@@ -118,9 +118,23 @@
     ]
 
 
-def coefficients_kernel(send_ref, swapped_ref, stayed_ref, leaf_ref, compress_ref, own_ref, out_ref, padded):
+def coefficients_kernel(
+    send_ref, swapped_ref, stayed_ref, leaf_ref, compress_ref, own_ref, got_ref, padded, packed, send_sem, recv_sem
+):
     leaves = own_ref.shape[0]
-    peers = out_ref.shape[0] // 16
+    peers = got_ref.shape[0] // 16
+    subs = lax.axis_size("sub")
+    me = lax.axis_index("space") * subs + lax.axis_index("sub")
+    barrier = pltpu.get_barrier_semaphore()
+
+    def greet(hop, carry):
+        peer = lax.rem(me + hop, peers)
+        pl.semaphore_signal(
+            barrier, inc=1, device_id=(peer // subs, lax.rem(peer, subs)), device_id_type=pl.DeviceIdType.MESH
+        )
+        return carry
+
+    lax.fori_loop(1, peers, greet, 0)
     total = jnp.zeros((leaves, 2 * RANK), jnp.float32)
     at = 0
     for sums in (swapped_ref, stayed_ref):
@@ -142,7 +156,7 @@
     row_of = lax.broadcasted_iota(jnp.int32, (8, 2 * RANK), 0)
     low = lax.broadcasted_iota(jnp.int32, (8, 2 * RANK), 1) < RANK
 
-    def pack(peer, carry):
+    def pack(peer):
         line = send_ref.at[pl.ds(peer * 32, 32)]
         halves = []
         for start in (0, 8):
@@ -152,10 +166,37 @@
                 both = jnp.where(low, padded[pl.ds(line[slot], 8), :], padded[pl.ds(line[slot + 1], 8), :])
                 rows = both if rows is None else jnp.where(row_of == j, both, rows)
             halves.append(rows)
-        out_ref[pl.ds(pl.multiple_of(peer * 16, 16), 16), :] = jnp.concatenate(halves, axis=0).astype(jnp.bfloat16)
+        return jnp.concatenate(halves, axis=0).astype(jnp.bfloat16)
+
+    def send(hop, carry):
+        peer = lax.rem(me + hop, peers)
+        at = pl.ds(pl.multiple_of(peer * 16, 16), 16)
+        packed[at, :] = pack(peer)
+        pltpu.make_async_remote_copy(
+            src_ref=packed.at[at, :],
+            dst_ref=got_ref.at[mine, :],
+            send_sem=send_sem,
+            recv_sem=recv_sem,
+            device_id=(peer // subs, lax.rem(peer, subs)),
+            device_id_type=pl.DeviceIdType.MESH,
+        ).start()
         return carry
 
-    lax.fori_loop(0, peers, pack, 0, unroll=4)
+    mine = pl.ds(pl.multiple_of(me * 16, 16), 16)
+    got_ref[mine, :] = pack(me)
+    pl.semaphore_wait(barrier, peers - 1)
+    lax.fori_loop(1, peers, send, 0)
+    others = pl.ds(0, (peers - 1) * 16)
+    everything = pltpu.make_async_remote_copy(
+        src_ref=packed.at[others, :],
+        dst_ref=got_ref.at[others, :],
+        send_sem=send_sem,
+        recv_sem=recv_sem,
+        device_id=(lax.axis_index("space"), lax.axis_index("sub")),
+        device_id_type=pl.DeviceIdType.MESH,
+    )
+    everything.wait_send()
+    everything.wait_recv()
 
 
 def translate_kernel(leaves, inter, src_ref, off_ref, own_ref, ghost_ref, kernels_ref, out_ref, tab, iota, held, placed, m2l_ref, sem):
@@ -404,7 +445,7 @@
     leaf_row = leaf_of_block.reshape(1, blocks)
     send = let_send.reshape(peers, per_peer) + 8 - (jnp.arange(per_peer, dtype=jnp.int32)[None, :] // 2) % 8
     vmem = pl.BlockSpec(memory_space=pltpu.VMEM)
-    own, outgoing = pl.pallas_call(
+    own, incoming = pl.pallas_call(
         coefficients_kernel,
         in_specs=[pl.BlockSpec(memory_space=pltpu.SMEM), vmem, vmem, vmem, vmem],
         out_specs=[vmem, vmem],
@@ -412,13 +453,15 @@
             jax.ShapeDtypeStruct((leaves, 2 * RANK), jnp.float32),
             jax.ShapeDtypeStruct((peers * per_peer // 2, 2 * RANK), jnp.bfloat16),
         ],
-        scratch_shapes=[pltpu.VMEM((leaves + 16, 2 * RANK), jnp.float32)],
-        compiler_params=params(),
+        scratch_shapes=[
+            pltpu.VMEM((leaves + 16, 2 * RANK), jnp.float32),
+            pltpu.VMEM((peers * per_peer // 2, 2 * RANK), jnp.bfloat16),
+            pltpu.SemaphoreType.DMA,
+            pltpu.SemaphoreType.DMA,
+        ],
+        compiler_params=params(collective_id=0, has_side_effects=True),
     )(send.reshape(-1), swapped, stayed, leaf_row, compress_polys)
-    incoming = lax.all_to_all(
-        outgoing.reshape(peers, per_peer // 2, 2 * RANK), ("space", "sub"), split_axis=0, concat_axis=0, tiled=True
-    )
-    local = translate(own, incoming.reshape(peers * per_peer // 2, 2 * RANK), inter_source, inter_offset, m2l_kernels)
+    local = translate(own, incoming, inter_source, inter_offset, m2l_kernels)
     values = pl.pallas_call(
         evaluate_kernel,
         grid=(regions,),

time: 175 us -> 171 us (0.977)
  Pallas kernels: 141 us -> 153 us
  waiting for transfers between devices: 9.61 us -> 0.01 us
  starting transfers between devices: 13.7 us -> 6.95 us
    pallas_call x1, Pallas kernels: 7.48 us -> 19.3 us  [on_device(): pl.pallas_call(coefficients_kernel, in_specs=[pl.BlockSpec(memory_space=p...]
    all_to_all x1 -> x0, waiting for transfers between devices: 9.6 us -> none  [on_device(): lax.all_to_all(outgoing.reshape(peers, per_peer // 2, 2 * RANK), ('space'...]
    all_to_all x1 -> x0, starting transfers between devices: 6.79 us -> none  [on_device(): lax.all_to_all(outgoing.reshape(peers, per_peer // 2, 2 * RANK), ('space'...]
    unnamed x26 -> x24, local copies, waits for them, and re-layouts: 3.65 us -> 2.91 us
  transfers between devices with their start and end apart: 4 -> 3, of which waited for: 1 -> 0; matrix products, arithmetic and copies ran while one was open for 4% -> 4% of each run, Pallas kernels for 5% -> 5%
where the time goes in v3:
time: 171 us; the launch traced here: 170 us
  Pallas kernels  153 us (89%)
  starting transfers between devices  6.95 us (4%)
  local copies, waits for them, and re-layouts  5.46 us (3%)
  other arithmetic  3.11 us (2%)
  matrix products  1.86 us (1%)
    pallas_call x1, Pallas kernels, translate(): pl.pallas_call(functools.partial(translate_kernel, leaves, inter), grid=(...  103 us
    pallas_call x1, Pallas kernels, on_device(): pl.pallas_call(coefficients_kernel, in_specs=[pl.BlockSpec(memory_space=p...  19.3 us
    pallas_call x1, Pallas kernels, on_device(): pl.pallas_call(evaluate_kernel, grid=(regions,), in_specs=[pl.BlockSpec((...  14.2 us
    pallas_call x1, Pallas kernels, on_device(): pl.pallas_call(moments_kernel, grid=(stays,), in_specs=[pl.BlockSpec(bloc...  9.31 us
    ppermute x3, starting transfers between devices, from_partner(): return lax.ppermute(block, axis, route)  6.95 us
    pallas_call x1, Pallas kernels, on_device(): pl.pallas_call(swapped_moments_kernel, grid=(SWAPS,), in_specs=[pl.BlockS...  6.63 us
  transfers between devices with their start and end apart: 3, of which 0 were waited for; matrix products, arithmetic and copies ran while one was open for 4% of the time, Pallas kernels for 5%

profile of v3, /device:TPU:1, one launch (start us, length us, event | category | flops | bytes accessed | tf_op | source)
XLA Modules:
  0.0 170.4 jit_solution(13604679491043435053)
XLA Ops:
  0.0 1.8 %copy.32 = f32[1,3,1024,128]{3,2,1,0:T(8,128)S(1)} copy(f32[1,3,1024,128]{3,1,2,0:T(4,128)} %bitcast.16) | data formatting | bytes 3145728
  1.8 0.0 copy-done.1
  1.8 0.7 fusion.2
  2.5 4.4 %collective-permute-start = (f32[4,128,128]{2,1,0:T(8,128)}, f32[4,128,128]{2,1,0:T(8,128)S(1)}, u32[]{:S(2)}, u32[]{:S(2)}) collective-permute-start(f32[4,128,128]{2,1,0:T(8,128)} %get-tuple-element.18), channel_id=1, source_target_pairs={{0,64},{64,0},{8,72},{72,8},{16,80},{80,16},{24,88},{88,24},{32,96... | collective-permute-start | bytes 786440 | tf_op jit(solution)/shard_map/ppermute | solution.py:34
  6.9 1.2 collective-permute-start.1
  8.2 1.3 collective-permute-start.2
  9.5 1.5 pad_maximum_fusion.bodies_ref
  11.0 0.0 copy-done
  11.0 0.9 convolution_bitcast_fusion.compress_ref
  11.9 0.2 broadcast_shift-right-arithmetic_fusion
  12.1 0.1 copy.26
  12.2 0.1 add.66
  12.3 0.1 sub.33
  12.4 0.2 copy.25
  12.7 0.2 copy.29
  13.0 0.0 copy-start.7
  13.0 0.0 copy-start.9
  13.0 1.1 reshape.97.src_ref
  14.1 0.6 sub.34.send_ref
  14.7 0.9 pad.9.off_ref
  15.6 9.3 %shard_map.119 = (f32[216,640]{1,0:T(8,128)}, f32[3,128,640]{2,1,0:T(8,128)}) custom-call(f32[4,1024,128]{2,1,0:T(8,128)} %pad_maximum_fusion.bodies_ref), custom_call_target="tpu_custom_call" | custom-call | flops 50000000 | bytes 4000000 | tf_op jit(solution)/shard_map/pallas_call | solution.py:409
  24.9 1.0 fusion.4.expand_ref
  25.9 0.0 collective-permute-done.got0_ref
  25.9 0.0 collective-permute-done.1.got1_ref
  25.9 0.0 collective-permute-done.2.got2_ref
  26.0 0.7 copy-done.4
  26.6 0.1 copy-done.5
  26.7 0.1 copy-done.6
  26.8 6.6 %shard_map.118 = (f32[216,384]{1,0:T(8,128)}, f32[3,128,384]{2,1,0:T(8,128)}) custom-call(s32[3]{0:T(128)} %bitcast.21, f32[4,1024,128]{2,1,0:T(8,128)} %pad_maximum_fusion.bodies_ref, f32[4,128,128]{2,1,0:T(8,128)} %copy-done.4, f32[4,128,128]{2,1,0:T(8,128)} %copy-done.5, f32[4,128,128]{2,1,0:T(8,128)} %copy-done.6), custom_call_target="tpu_custom_call" | custom-call | tf_op jit(solution)/shard_map/pallas_call | solution.py:423
  33.5 19.3 %shard_map.120 = (f32[640,128]{1,0:T(8,128)}, bf16[2048,128]{1,0:T(8,128)(2,1)}) custom-call(s32[4096]{0:T(1024)} %sub.34.send_ref, f32[216,384]{1,0:T(8,128)} %get-tuple-element.13.swapped_ref, f32[216,640]{1,0:T(8,128)} %get-tuple-element.14.stayed_ref, s32[1,1024]{1,0:T(1,128)} %bitcast.19, f32[64,216]{1,0:T(8,128)} %convolution_bitcast_fusion.compress_ref), custom_call_target="tpu_custom_call" | custom-call | tf_op jit(solution)/shard_map/pallas_call | solution.py:448
  52.8 103.4 %shard_map.121.local_ref = f32[640,64]{1,0:T(8,128)} custom-call(s32[122880]{0:T(1024)} %reshape.97.src_ref, f32[640,256]{1,0:T(8,128)} %pad.9.off_ref, f32[640,128]{1,0:T(8,128)} %get-tuple-element.15.own_ref, bf16[2048,128]{1,0:T(8,128)(2,1)} %get-tuple-element.16.ghost_ref, bf16[64,20224]{1,0:T(8,128)(2,1)} %kernels_ref.1), custom_call_target="tpu_custom_call" | custom-call | tf_op jit(solution)/shard_map/pallas_call | solution.py:308
  156.2 14.2 %shard_map.122 = f32[1024,128]{1,0:T(8,128)} custom-call(f32[3,128,384]{2,1,0:T(8,128)} %get-tuple-element.11.swapped_ref, f32[3,128,640]{2,1,0:T(8,128)} %get-tuple-element.12.stayed_ref, s32[1,1024]{1,0:T(1,128)} %bitcast.20, f32[640,64]{1,0:T(8,128)} %shard_map.121.local_ref, f32[216,64]{1,0:T(8,128)} %fusion.4.expand_ref), custom_call_target="tpu_custom_call" | custom-call | tf_op jit(solution)/shard_map/pallas_call | solution.py:465
  (21 shorter events, 0.1 us)
Async XLA Ops:
  0.0 11.0 %copy-start = (f32[216,64]{0,1:T(8,128)S(1)}, f32[216,64]{0,1:T(8,128)}, u32[]{:S(2)}) copy-start(f32[216,64]{0,1:T(8,128)} %param.19) | copy-start | bytes 165892
  0.0 1.8 %copy-start.1 = (f32[131072]{0:T(1024)S(1)}, f32[131072]{0:T(1024)}, u32[]{:S(2)}) copy-start(f32[131072]{0:T(1024)} %param.13) | copy-start | bytes 1572868
  2.5 23.4 %collective-permute-start = (f32[4,128,128]{2,1,0:T(8,128)}, f32[4,128,128]{2,1,0:T(8,128)S(1)}, u32[]{:S(2)}, u32[]{:S(2)}) collective-permute-start(f32[4,128,128]{2,1,0:T(8,128)} %get-tuple-element.18), channel_id=1, source_target_pairs={{0,64},{64,0},{8,72},{72,8},{16,80},{80,16},{24,88},{88,24},{32,96... | collective-permute-start | bytes 786440 | tf_op jit(solution)/shard_map/ppermute | solution.py:34
  6.9 19.0 %collective-permute-start.1 = (f32[4,128,128]{2,1,0:T(8,128)S(1)}, f32[4,128,128]{2,1,0:T(8,128)S(1)}, u32[]{:S(2)}, u32[]{:S(2)}) collective-permute-start(f32[4,128,128]{2,1,0:T(8,128)S(1)} %get-tuple-element.19), channel_id=1, source_target_pairs={{0,8},{8,0},{16,24},{24,16},{32,40},{40,32},{48,56},{56,48},{64,72... | collective-permute-start | bytes 786440 | tf_op jit(solution)/shard_map/ppermute | solution.py:34
  8.2 2.8 %copy-start.10 = (s32[1,128,32]{1,2,0:T(8,128)S(1)}, s32[1,128,32]{1,2,0:T(8,128)}, u32[]{:S(2)}) copy-start(s32[1,128,32]{1,2,0:T(8,128)} %param.16) | copy-start | bytes 49156
  8.2 2.8 %copy-start.8 = (f32[216,216]{1,0:T(8,128)S(1)}, f32[216,216]{1,0:T(8,128)}, u32[]{:S(2)}) copy-start(f32[216,216]{1,0:T(8,128)} %constant.58.clone) | copy-start | bytes 559876
  8.2 3.7 %copy-start.2 = (s32[640,189]{0,1:T(8,128)S(1)}, s32[640,189]{0,1:T(8,128)}, u32[]{:S(2)}) copy-start(s32[640,189]{0,1:T(8,128)} %param.18) | copy-start | bytes 1451524
  8.2 3.7 %copy-start.3 = (s32[640,189]{0,1:T(8,128)S(1)}, s32[640,189]{0,1:T(8,128)}, u32[]{:S(2)}) copy-start(s32[640,189]{0,1:T(8,128)} %param.17) | copy-start | bytes 1451524
  8.2 17.8 %collective-permute-start.2 = (f32[4,128,128]{2,1,0:T(8,128)S(1)}, f32[4,128,128]{2,1,0:T(8,128)S(1)}, u32[]{:S(2)}, u32[]{:S(2)}) collective-permute-start(f32[4,128,128]{2,1,0:T(8,128)S(1)} %get-tuple-element.17), channel_id=1, source_target_pairs={{0,1},{1,0},{2,3},{3,2},{4,5},{5,4},{6,7},{7,6},{8,9},{9,8},{10,11... | collective-permute-start | bytes 786440 | tf_op jit(solution)/shard_map/ppermute | solution.py:34
  13.0 12.0 %copy-start.7 = (f32[216,216]{1,0:T(8,128)S(1)}, f32[216,216]{1,0:T(8,128)}, u32[]{:S(2)}) copy-start(f32[216,216]{1,0:T(8,128)} %constant.59.clone) | copy-start | bytes 559876
  13.0 11.9 %copy-start.9 = (f32[64,216]{1,0:T(8,128)S(1)}, f32[64,216]{1,0:T(8,128)}, u32[]{:S(2)}) copy-start(f32[64,216]{1,0:T(8,128)} %param.21) | copy-start | bytes 165892
  25.9 0.7 copy-start.4
  25.9 0.8 copy-start.5
  25.9 0.9 copy-start.6

commit v4 on v3

--- a/solution.py
+++ b/solution.py
@@ -18,6 +18,7 @@
 PAIRS = 160
 PITCH = 81
 UNROLL = 8
+STRIDE = 9
 
 
 def params(**more):
@@ -55,11 +56,11 @@
     return first, (values - first.astype(jnp.float32)).astype(jnp.bfloat16)
 
 
-def gather_moments(bodies, out_ref, turned_ref, px, py, pz, partial):
-    mass = bodies[3].T
+def gather_moments(coords, masses, out_ref, turned_ref, px, py, pz, partial):
+    mass = masses[...].T
     px[0] = mass
     for dim, scratch in enumerate((px, py, pz)):
-        points = bodies[dim].T
+        points = coords[dim].T
         turned_ref[dim] = points
         for k, poly in enumerate(chebyshev(points)):
             scratch[k + 1] = poly * mass if dim == 0 else poly
@@ -80,23 +81,36 @@
         zero = jnp.zeros((8, REGION), jnp.float32)
         sums = lax.fori_loop(0, BLOCK // 8, chunk, (zero,) * (ORDER * ORDER), unroll=4)
         for n in range(ORDER * ORDER):
-            partial[pl.ds(pl.multiple_of((i * ORDER * ORDER + n) * 8, 8), 8), :] = sums[n]
+            partial[pl.ds((i * ORDER * ORDER + n) * STRIDE, 8), :] = sums[n]
         return carry
 
     lax.fori_loop(0, ORDER, along, 0)
     count = out_ref.shape[0]
-    total = partial[pl.ds(0, count, stride=8), :]
+    total = partial[pl.ds(0, count, stride=STRIDE), :]
     for s in range(1, 8):
-        total += partial[pl.ds(s, count, stride=8), :]
+        total += partial[pl.ds(s, count, stride=STRIDE), :]
     out_ref[...] = total
 
 
-def moments_kernel(bodies_ref, out_ref, turned_ref, px, py, pz, partial):
-    gather_moments(bodies_ref, out_ref, turned_ref, px, py, pz, partial)
+def moments_kernel(coords_ref, masses_ref, out_ref, turned_ref, px, py, pz, partial):
+    gather_moments(coords_ref, masses_ref, out_ref, turned_ref, px, py, pz, partial)
 
 
 def swapped_moments_kernel(
-    counts_ref, bodies_ref, got0_ref, got1_ref, got2_ref, out_ref, turned_ref, merged, px, py, pz, partial
+    counts_ref,
+    coords_ref,
+    masses_ref,
+    got0_ref,
+    got1_ref,
+    got2_ref,
+    out_ref,
+    turned_ref,
+    coords,
+    masses,
+    px,
+    py,
+    pz,
+    partial,
 ):
     column = lax.broadcasted_iota(jnp.int32, (REGION, BLOCK), 0) * BLOCK + lax.broadcasted_iota(
         jnp.int32, (REGION, BLOCK), 1
@@ -106,15 +120,16 @@
         @pl.when(pl.program_id(0) == rnd)
         def _():
             keep = column < counts_ref[rnd]
-            for dim in range(4):
-                merged[dim] = jnp.where(keep, got[dim], bodies_ref[dim])
-
-    gather_moments(merged, out_ref, turned_ref, px, py, pz, partial)
+            for dim in range(3):
+                coords[dim] = jnp.where(keep, got[dim], coords_ref[dim])
+            masses[...] = jnp.where(keep, got[3], masses_ref[...])
+
+    gather_moments(coords, masses, out_ref, turned_ref, px, py, pz, partial)
 
 
 def moment_scratch(nodes_count):
     return [pltpu.VMEM((ORDER, BLOCK, REGION), jnp.float32) for _ in range(3)] + [
-        pltpu.VMEM((8 * nodes_count, REGION), jnp.float32)
+        pltpu.VMEM((STRIDE * nodes_count, REGION), jnp.float32)
     ]
 
 
@@ -253,7 +268,7 @@
         line = jnp.broadcast_to(off_ref[pl.ds(cell, 1), :], (16, 256)).astype(jnp.bfloat16)
         line = jnp.concatenate([line] * (PAIRS // 16), axis=0)
         chosen = jnp.where(iota[...] == line, jnp.bfloat16(1), jnp.bfloat16(0))
-        return jnp.dot(chosen, rows_of, preferred_element_type=jnp.float32)
+        return jnp.dot(chosen[:, :SLOTS], rows_of, preferred_element_type=jnp.float32)
 
     def contract(tile, count):
         pieces = []
@@ -320,7 +335,7 @@
         scratch_shapes=[
             pltpu.VMEM((2 * rows + 16, 128), jnp.float32),
             pltpu.VMEM((PAIRS, 256), jnp.bfloat16),
-            pltpu.VMEM((UNROLL, 256, 128), jnp.bfloat16),
+            pltpu.VMEM((UNROLL, SLOTS, 128), jnp.bfloat16),
             pltpu.VMEM((2 * PAIRS * PITCH, 128), jnp.float32),
             pltpu.VMEM((RANK, PAIRS * 128), jnp.bfloat16),
             pltpu.SemaphoreType.DMA,
@@ -332,24 +347,23 @@
 def evaluate_kernel(swapped_ref, stayed_ref, leaf_ref, local_ref, expand_ref, out_ref, bodies, nodes, result):
     step = pl.program_id(0)
     leaves = local_ref.shape[0]
-    count = expand_ref.shape[0]
 
     @pl.when(step == 0)
     def _():
-        full = lax.dot_general(
-            expand_ref[...],
-            local_ref[...],
-            (((1,), (1,)), ((), ())),
-            precision=lax.Precision.HIGHEST,
-            preferred_element_type=jnp.float32,
-        )
-        parts = jnp.concatenate(split_two(full), axis=0)
-        for region in range(nodes.shape[0]):
-            ids = leaf_ref[:, pl.ds(region * REGION, REGION)]
-            onehot = lax.broadcasted_iota(jnp.int32, (leaves, REGION), 0) == ids
+        local = jnp.concatenate([part.astype(jnp.float32) for part in split_two(local_ref[...])], axis=1)
+        local = local.T.astype(jnp.bfloat16)
+        large, small = split_two(expand_ref[...])
+        expands = jnp.concatenate([large, large, small], axis=1)
+        width = 2 * REGION
+        for pair in range(nodes.shape[0] // 2):
+            ids = leaf_ref[:, pl.ds(pair * width, width)]
+            onehot = lax.broadcasted_iota(jnp.int32, (leaves, width), 0) == ids
             onehot = jnp.where(onehot, 1.0, 0.0).astype(jnp.bfloat16)
-            picked = jnp.dot(parts, onehot, preferred_element_type=jnp.float32)
-            nodes[region] = picked[:count] + picked[count:]
+            picked = jnp.dot(local, onehot, preferred_element_type=jnp.float32).astype(jnp.bfloat16)
+            terms = jnp.concatenate([picked, picked[:RANK]], axis=0)
+            values = jnp.dot(expands, terms, preferred_element_type=jnp.float32)
+            nodes[2 * pair] = values[:, :REGION]
+            nodes[2 * pair + 1] = values[:, REGION:]
 
     @pl.when(step < SWAPS)
     def _():
@@ -397,19 +411,25 @@
     blocks = local_bodies // BLOCK
     regions = blocks // REGION
     peers, per_peer = let_send.shape[1:]
-    bodies = jnp.concatenate([coords.reshape(3, blocks, BLOCK), masses.reshape(1, blocks, BLOCK)], axis=0)
+    coords = coords.reshape(3, blocks, BLOCK)
+    masses = masses.reshape(blocks, BLOCK)
     top_bit = lax.axis_size("space").bit_length() - 2
-    got_outer = from_partner(bodies[:, 0:REGION], "space", top_bit)
-    got_inner = from_partner(bodies[:, REGION : 2 * REGION], "space", 0)
-    got_sub = from_partner(bodies[:, 2 * REGION : 3 * REGION], "sub", 0)
-    block4 = (4, REGION, BLOCK)
+    got = []
+    for rnd, (axis, distance) in enumerate((("space", top_bit), ("space", 0), ("sub", 0))):
+        at = slice(rnd * REGION, (rnd + 1) * REGION)
+        got.append(from_partner(jnp.concatenate([coords[:, at], masses[None, at]], axis=0), axis, distance))
+    coords_block = (3, REGION, BLOCK)
+    masses_block = (REGION, BLOCK)
     sums_spec = pl.BlockSpec((nodes_count, REGION), lambda g: (0, g))
     turned_spec = pl.BlockSpec((3, BLOCK, REGION), lambda g: (0, 0, g))
     stays = regions - SWAPS
     stayed, stayed_turned = pl.pallas_call(
         moments_kernel,
         grid=(stays,),
-        in_specs=[pl.BlockSpec(block4, lambda g: (0, g + SWAPS, 0))],
+        in_specs=[
+            pl.BlockSpec(coords_block, lambda g: (0, g + SWAPS, 0)),
+            pl.BlockSpec(masses_block, lambda g: (g + SWAPS, 0)),
+        ],
         out_specs=[sums_spec, turned_spec],
         out_shape=[
             jax.ShapeDtypeStruct((nodes_count, stays * REGION), jnp.float32),
@@ -418,14 +438,15 @@
         scratch_shapes=moment_scratch(nodes_count),
         compiler_params=params(),
         cost_estimate=pl.CostEstimate(flops=50_000_000, bytes_accessed=4_000_000, transcendentals=0),
-    )(bodies)
-    whole4 = pl.BlockSpec(block4, lambda g: (0, 0, 0))
+    )(coords, masses)
+    whole4 = pl.BlockSpec((4, REGION, BLOCK), lambda g: (0, 0, 0))
     swapped, swapped_turned = pl.pallas_call(
         swapped_moments_kernel,
         grid=(SWAPS,),
         in_specs=[
             pl.BlockSpec(memory_space=pltpu.SMEM),
-            pl.BlockSpec(block4, lambda g: (0, g, 0)),
+            pl.BlockSpec(coords_block, lambda g: (0, g, 0)),
+            pl.BlockSpec(masses_block, lambda g: (g, 0)),
             whole4,
             whole4,
             whole4,
@@ -435,9 +456,10 @@
             jax.ShapeDtypeStruct((nodes_count, SWAPS * REGION), jnp.float32),
             jax.ShapeDtypeStruct((3, BLOCK, SWAPS * REGION), jnp.float32),
         ],
-        scratch_shapes=[pltpu.VMEM(block4, jnp.float32)] + moment_scratch(nodes_count),
+        scratch_shapes=[pltpu.VMEM(coords_block, jnp.float32), pltpu.VMEM(masses_block, jnp.float32)]
+        + moment_scratch(nodes_count),
         compiler_params=params(),
-    )(swap_counts.reshape(SWAPS), bodies, got_outer, got_inner, got_sub)
+    )(swap_counts.reshape(SWAPS), coords, masses, *got)
     basis = node_basis()
     exact = functools.partial(jnp.dot, precision=lax.Precision.HIGHEST, preferred_element_type=jnp.float32)
     compress_polys = exact(compress.T, basis)

time: 171 us -> 170 us (level)
  Pallas kernels: 153 us -> 151 us
where the time goes in v4:
time: 170 us
  Pallas kernels  151 us (89%)
  local copies, waits for them, and re-layouts  7.06 us (4%)
  starting transfers between devices  6.87 us (4%)
  other arithmetic  3.02 us (2%)
  matrix products  1.87 us (1%)
    pallas_call x1, Pallas kernels, translate(): pl.pallas_call(functools.partial(translate_kernel, leaves, inter), grid=(...  102 us
    pallas_call x1, Pallas kernels, on_device(): pl.pallas_call(coefficients_kernel, in_specs=[pl.BlockSpec(memory_space=p...  19.3 us
    pallas_call x1, Pallas kernels, on_device(): pl.pallas_call(evaluate_kernel, grid=(regions,), in_specs=[pl.BlockSpec((...  13.3 us
    pallas_call x1, Pallas kernels, on_device(): pl.pallas_call(moments_kernel, grid=(stays,), in_specs=[pl.BlockSpec(coor...  8.96 us
    ppermute x3, starting transfers between devices, from_partner(): return lax.ppermute(block, axis, route)  6.87 us
    pallas_call x1, Pallas kernels, on_device(): pl.pallas_call(swapped_moments_kernel, grid=(SWAPS,), in_specs=[pl.BlockS...  6.55 us
  transfers between devices with their start and end apart: 3, of which 0 were waited for; matrix products, arithmetic and copies ran while one was open for 4% of the time, Pallas kernels for 5%

profile of v4, /device:TPU:1, one launch (start us, length us, event | category | flops | bytes accessed | tf_op | source)
XLA Modules:
  0.0 169.6 jit_solution(7445189993128061473)
XLA Ops:
  0.0 1.7 %copy.32 = f32[1,3,1024,128]{3,2,1,0:T(8,128)S(1)} copy(f32[1,3,1024,128]{3,1,2,0:T(4,128)} %bitcast.25) | data formatting | bytes 3145728
  1.7 0.0 copy-start.10
  1.8 0.0 copy-start.8
  1.8 0.0 copy-start.2
  1.8 0.0 copy-start.3
  1.8 1.6 slice_bitcast_fusion
  3.4 0.7 pad_maximum_fusion
  4.1 4.4 %collective-permute-start = (f32[4,128,128]{2,1,0:T(8,128)}, f32[4,128,128]{2,1,0:T(8,128)S(1)}, u32[]{:S(2)}, u32[]{:S(2)}) collective-permute-start(f32[4,128,128]{2,1,0:T(8,128)} %pad_maximum_fusion), channel_id=1, source_target_pairs={{0,64},{64,0},{8,72},{72,8},{16,80},{80,16},{24,88},{88,24},{32,96... | collective-permute-start | bytes 786440 | tf_op jit(solution)/shard_map/ppermute | solution.py:35
  8.6 0.7 pad_maximum_fusion.1
  9.3 1.2 collective-permute-start.1
  10.5 0.7 pad_maximum_fusion.2
  11.2 1.2 collective-permute-start.2
  12.5 0.9 convolution_bitcast_fusion.compress_ref
  13.3 0.2 broadcast_shift-right-arithmetic_fusion
  13.6 0.1 copy.26
  13.7 0.1 add.66
  13.8 0.1 sub.33
  13.9 0.2 copy.25
  14.2 0.2 copy.29
  14.4 0.0 copy-start.7
  14.5 1.1 reshape.127.src_ref
  15.6 0.6 sub.34.send_ref
  16.2 0.9 pad.9.off_ref
  17.1 9.0 %shard_map.119 = (f32[216,640]{1,0:T(8,128)}, f32[3,128,640]{2,1,0:T(8,128)}) custom-call(f32[3,1024,128]{2,1,0:T(8,128)} %bitcast.21, f32[1024,128]{1,0:T(8,128)} %bitcast.23), custom_call_target="tpu_custom_call" | custom-call | flops 50000000 | bytes 4000000 | tf_op jit(solution)/shard_map/pallas_call | solution.py:426
  26.1 1.0 fusion.2.expand_ref
  27.1 0.7 copy-done.4
  27.8 0.1 copy-done.5
  27.9 0.1 copy-done.6
  28.0 6.6 %shard_map.118 = (f32[216,384]{1,0:T(8,128)}, f32[3,128,384]{2,1,0:T(8,128)}) custom-call(s32[3]{0:T(128)} %bitcast.28, f32[3,1024,128]{2,1,0:T(8,128)} %bitcast.22, f32[1024,128]{1,0:T(8,128)} %bitcast.24, f32[4,128,128]{2,1,0:T(8,128)} %copy-done.4, f32[4,128,128]{2,1,0:T(8,128)} %copy-done.5, f32[4,128,128]{2,1,0:T(8,128)} %copy-done.6), custom_call_target="tpu_custom_call" | custom-call | tf_op jit(solution)/shard_map/pallas_call | solution.py:443
  34.5 19.3 %shard_map.120 = (f32[640,128]{1,0:T(8,128)}, bf16[2048,128]{1,0:T(8,128)(2,1)}) custom-call(s32[4096]{0:T(1024)} %sub.34.send_ref, f32[216,384]{1,0:T(8,128)} %get-tuple-element.13.swapped_ref, f32[216,640]{1,0:T(8,128)} %get-tuple-element.14.stayed_ref, s32[1,1024]{1,0:T(1,128)} %bitcast.26, f32[64,216]{1,0:T(8,128)} %convolution_bitcast_fusion.compress_ref), custom_call_target="tpu_custom_call" | custom-call | tf_op jit(solution)/shard_map/pallas_call | solution.py:470
  53.8 102.4 %shard_map.121.local_ref = f32[640,64]{1,0:T(8,128)} custom-call(s32[122880]{0:T(1024)} %reshape.127.src_ref, f32[640,256]{1,0:T(8,128)} %pad.9.off_ref, f32[640,128]{1,0:T(8,128)} %get-tuple-element.15.own_ref, bf16[2048,128]{1,0:T(8,128)(2,1)} %get-tuple-element.16.ghost_ref, bf16[64,20224]{1,0:T(8,128)(2,1)} %kernels_ref.1), custom_call_target="tpu_custom_call" | custom-call | tf_op jit(solution)/shard_map/pallas_call | solution.py:323
  156.3 13.3 %shard_map.122 = f32[1024,128]{1,0:T(8,128)} custom-call(f32[3,128,384]{2,1,0:T(8,128)} %get-tuple-element.11.swapped_ref, f32[3,128,640]{2,1,0:T(8,128)} %get-tuple-element.12.stayed_ref, s32[1,1024]{1,0:T(1,128)} %bitcast.27, f32[640,64]{1,0:T(8,128)} %shard_map.121.local_ref, f32[216,64]{1,0:T(8,128)} %fusion.2.expand_ref), custom_call_target="tpu_custom_call" | custom-call | tf_op jit(solution)/shard_map/pallas_call | solution.py:487
  (24 shorter events, 0.2 us)
Async XLA Ops:
  0.0 12.4 %copy-start = (f32[216,64]{0,1:T(8,128)S(1)}, f32[216,64]{0,1:T(8,128)}, u32[]{:S(2)}) copy-start(f32[216,64]{0,1:T(8,128)} %param.19) | copy-start | bytes 165892
  1.7 11.8 %copy-start.1 = (f32[1,3,1024,128]{3,2,1,0:T(8,128)}, f32[1,3,1024,128]{3,2,1,0:T(8,128)S(1)}, u32[]{:S(2)}) copy-start(f32[1,3,1024,128]{3,2,1,0:T(8,128)S(1)} %copy.32) | copy-start | bytes 4718596
  1.7 10.7 %copy-start.10 = (s32[1,128,32]{1,2,0:T(8,128)S(1)}, s32[1,128,32]{1,2,0:T(8,128)}, u32[]{:S(2)}) copy-start(s32[1,128,32]{1,2,0:T(8,128)} %param.16) | copy-start | bytes 49156
  1.8 10.7 %copy-start.8 = (f32[216,216]{1,0:T(8,128)S(1)}, f32[216,216]{1,0:T(8,128)}, u32[]{:S(2)}) copy-start(f32[216,216]{1,0:T(8,128)} %constant.58.clone) | copy-start | bytes 559876
  1.8 11.6 %copy-start.2 = (s32[640,189]{0,1:T(8,128)S(1)}, s32[640,189]{0,1:T(8,128)}, u32[]{:S(2)}) copy-start(s32[640,189]{0,1:T(8,128)} %param.18) | copy-start | bytes 1451524
  1.8 11.6 %copy-start.3 = (s32[640,189]{0,1:T(8,128)S(1)}, s32[640,189]{0,1:T(8,128)}, u32[]{:S(2)}) copy-start(s32[640,189]{0,1:T(8,128)} %param.17) | copy-start | bytes 1451524
  4.1 22.9 %collective-permute-start = (f32[4,128,128]{2,1,0:T(8,128)}, f32[4,128,128]{2,1,0:T(8,128)S(1)}, u32[]{:S(2)}, u32[]{:S(2)}) collective-permute-start(f32[4,128,128]{2,1,0:T(8,128)} %pad_maximum_fusion), channel_id=1, source_target_pairs={{0,64},{64,0},{8,72},{72,8},{16,80},{80,16},{24,88},{88,24},{32,96... | collective-permute-start | bytes 786440 | tf_op jit(solution)/shard_map/ppermute | solution.py:35
  9.3 17.8 %collective-permute-start.1 = (f32[4,128,128]{2,1,0:T(8,128)}, f32[4,128,128]{2,1,0:T(8,128)S(1)}, u32[]{:S(2)}, u32[]{:S(2)}) collective-permute-start(f32[4,128,128]{2,1,0:T(8,128)} %pad_maximum_fusion.1), channel_id=1, source_target_pairs={{0,8},{8,0},{16,24},{24,16},{32,40},{40,32},{48,56},{56,48},{64,72... | collective-permute-start | bytes 786440 | tf_op jit(solution)/shard_map/ppermute | solution.py:35
  11.2 15.9 %collective-permute-start.2 = (f32[4,128,128]{2,1,0:T(8,128)}, f32[4,128,128]{2,1,0:T(8,128)S(1)}, u32[]{:S(2)}, u32[]{:S(2)}) collective-permute-start(f32[4,128,128]{2,1,0:T(8,128)} %pad_maximum_fusion.2), channel_id=1, source_target_pairs={{0,1},{1,0},{2,3},{3,2},{4,5},{5,4},{6,7},{7,6},{8,9},{9,8},{10,11... | collective-permute-start | bytes 786440 | tf_op jit(solution)/shard_map/ppermute | solution.py:35
  14.4 11.6 %copy-start.7 = (f32[216,216]{1,0:T(8,128)S(1)}, f32[216,216]{1,0:T(8,128)}, u32[]{:S(2)}) copy-start(f32[216,216]{1,0:T(8,128)} %constant.59.clone) | copy-start | bytes 559876
  14.5 11.6 %copy-start.9 = (f32[64,216]{1,0:T(8,128)S(1)}, f32[64,216]{1,0:T(8,128)}, u32[]{:S(2)}) copy-start(f32[64,216]{1,0:T(8,128)} %param.21) | copy-start | bytes 165892
  27.0 0.7 copy-start.4
  27.1 0.8 copy-start.5
  27.1 0.9 copy-start.6

commit v5 on v4

--- a/solution.py
+++ b/solution.py
@@ -23,16 +23,6 @@
 
 def params(**more):
     return pltpu.CompilerParams(vmem_limit_bytes=56 << 20, **more)
-
-
-def from_partner(block, axis, distance):
-    count = lax.axis_size(axis)
-    route = []
-    for low in range(count):
-        high = low | 1 << distance
-        if high != low and high < count:
-            route += [(low, high), (high, low)]
-    return lax.ppermute(block, axis, route)
 
 
 def chebyshev(points):
@@ -92,39 +82,85 @@
     out_ref[...] = total
 
 
-def moments_kernel(coords_ref, masses_ref, out_ref, turned_ref, px, py, pz, partial):
-    gather_moments(coords_ref, masses_ref, out_ref, turned_ref, px, py, pz, partial)
-
-
-def swapped_moments_kernel(
+def moments_kernel(
     counts_ref,
     coords_ref,
     masses_ref,
-    got0_ref,
-    got1_ref,
-    got2_ref,
+    all_coords,
+    all_masses,
     out_ref,
     turned_ref,
     coords,
     masses,
+    got,
+    send_sem,
+    recv_sem,
     px,
     py,
     pz,
     partial,
 ):
+    step = pl.program_id(0)
+    stays = pl.num_programs(0) - SWAPS
+    space, sub = lax.axis_index("space"), lax.axis_index("sub")
+    spaces = lax.axis_size("space")
+    partners = (
+        (lax.rem(space + spaces // 2, spaces), sub),
+        (space + 1 - 2 * lax.rem(space, 2), sub),
+        (space, sub + 1 - 2 * lax.rem(sub, 2)),
+    )
     column = lax.broadcasted_iota(jnp.int32, (REGION, BLOCK), 0) * BLOCK + lax.broadcasted_iota(
         jnp.int32, (REGION, BLOCK), 1
     )
-    for rnd, got in enumerate((got0_ref, got1_ref, got2_ref)):
-
-        @pl.when(pl.program_id(0) == rnd)
+
+    def copies(rnd):
+        at = pl.ds(rnd * REGION, REGION)
+        pairs = ((all_coords.at[:, at, :], got.at[rnd, pl.ds(0, 3)]), (all_masses.at[at, :], got.at[rnd, 3]))
+        return [
+            pltpu.make_async_remote_copy(
+                src_ref=source,
+                dst_ref=target,
+                send_sem=send_sem.at[2 * rnd + k],
+                recv_sem=recv_sem.at[2 * rnd + k],
+                device_id=partners[rnd],
+                device_id_type=pl.DeviceIdType.MESH,
+            )
+            for k, (source, target) in enumerate(pairs)
+        ]
+
+    @pl.when(step == 0)
+    def _():
+        barrier = pltpu.get_barrier_semaphore()
+        for partner in partners:
+            pl.semaphore_signal(barrier, inc=1, device_id=partner, device_id_type=pl.DeviceIdType.MESH)
+        pl.semaphore_wait(barrier, SWAPS)
+        for rnd in range(SWAPS):
+            for copy in copies(rnd):
+                copy.start()
+
+    @pl.when(step < stays)
+    def _():
+        coords[...] = coords_ref[...]
+        masses[...] = masses_ref[...]
+
+    for rnd in range(SWAPS):
+
+        @pl.when(step == stays + rnd)
         def _():
+            for copy in copies(rnd):
+                copy.wait_recv()
             keep = column < counts_ref[rnd]
             for dim in range(3):
-                coords[dim] = jnp.where(keep, got[dim], coords_ref[dim])
-            masses[...] = jnp.where(keep, got[3], masses_ref[...])
+                coords[dim] = jnp.where(keep, got[rnd, dim], coords_ref[dim])
+            masses[...] = jnp.where(keep, got[rnd, 3], masses_ref[...])
 
     gather_moments(coords, masses, out_ref, turned_ref, px, py, pz, partial)
+
+    @pl.when(step == stays + SWAPS - 1)
+    def _():
+        for rnd in range(SWAPS):
+            for copy in copies(rnd):
+                copy.wait_send()
 
 
 def moment_scratch(nodes_count):
@@ -134,7 +170,7 @@
 
 
 def coefficients_kernel(
-    send_ref, swapped_ref, stayed_ref, leaf_ref, compress_ref, own_ref, got_ref, padded, packed, send_sem, recv_sem
+    send_ref, sums_ref, leaf_ref, compress_ref, own_ref, got_ref, padded, packed, send_sem, recv_sem
 ):
     leaves = own_ref.shape[0]
     peers = got_ref.shape[0] // 16
@@ -150,19 +186,13 @@
         return carry
 
     lax.fori_loop(1, peers, greet, 0)
-    total = jnp.zeros((leaves, 2 * RANK), jnp.float32)
-    at = 0
-    for sums in (swapped_ref, stayed_ref):
-        count = sums.shape[1]
-        ids = leaf_ref[:, pl.ds(at, count)]
-        onehot = lax.broadcasted_iota(jnp.int32, (leaves, count), 0) == ids
-        onehot = jnp.where(onehot, 1.0, 0.0).astype(jnp.bfloat16)
-        moved = jnp.dot(
-            compress_ref[...], sums[...], precision=lax.Precision.HIGHEST, preferred_element_type=jnp.float32
-        )
-        both = jnp.concatenate(split_two(moved), axis=0)
-        total += lax.dot_general(onehot, both, (((1,), (1,)), ((), ())), preferred_element_type=jnp.float32)
-        at += count
+    onehot = lax.broadcasted_iota(jnp.int32, (leaves, leaf_ref.shape[1]), 0) == leaf_ref[...]
+    onehot = jnp.where(onehot, 1.0, 0.0).astype(jnp.bfloat16)
+    moved = jnp.dot(
+        compress_ref[...], sums_ref[...], precision=lax.Precision.HIGHEST, preferred_element_type=jnp.float32
+    )
+    both = jnp.concatenate(split_two(moved), axis=0)
+    total = lax.dot_general(onehot, both, (((1,), (1,)), ((), ())), preferred_element_type=jnp.float32)
     own = (total + pltpu.roll(total, RANK, 1)).astype(jnp.bfloat16).astype(jnp.float32)
     own_ref[...] = own
     padded[pl.ds(0, 8), :] = jnp.zeros((8, 2 * RANK), jnp.float32)
@@ -344,7 +374,7 @@
     )(row, pair, own, ghost, m2l_kernels)
 
 
-def evaluate_kernel(swapped_ref, stayed_ref, leaf_ref, local_ref, expand_ref, out_ref, bodies, nodes, result):
+def evaluate_kernel(turned_ref, leaf_ref, local_ref, expand_ref, out_ref, nodes, result):
     step = pl.program_id(0)
     leaves = local_ref.shape[0]
 
@@ -365,17 +395,9 @@
             nodes[2 * pair] = values[:, :REGION]
             nodes[2 * pair + 1] = values[:, REGION:]
 
-    @pl.when(step < SWAPS)
-    def _():
-        bodies[...] = swapped_ref[...]
-
-    @pl.when(step >= SWAPS)
-    def _():
-        bodies[...] = stayed_ref[...]
-
     def chunk(v, carry):
         at = pl.ds(pl.multiple_of(v * 16, 16), 16)
-        px, py, pz = (chebyshev(bodies[dim, at, :]) for dim in range(3))
+        px, py, pz = (chebyshev(turned_ref[dim, at, :]) for dim in range(3))
         value = None
         for i in range(ORDER):
             middle = None
@@ -413,53 +435,40 @@
     peers, per_peer = let_send.shape[1:]
     coords = coords.reshape(3, blocks, BLOCK)
     masses = masses.reshape(blocks, BLOCK)
-    top_bit = lax.axis_size("space").bit_length() - 2
-    got = []
-    for rnd, (axis, distance) in enumerate((("space", top_bit), ("space", 0), ("sub", 0))):
-        at = slice(rnd * REGION, (rnd + 1) * REGION)
-        got.append(from_partner(jnp.concatenate([coords[:, at], masses[None, at]], axis=0), axis, distance))
-    coords_block = (3, REGION, BLOCK)
-    masses_block = (REGION, BLOCK)
-    sums_spec = pl.BlockSpec((nodes_count, REGION), lambda g: (0, g))
-    turned_spec = pl.BlockSpec((3, BLOCK, REGION), lambda g: (0, 0, g))
-    stays = regions - SWAPS
-    stayed, stayed_turned = pl.pallas_call(
+    hbm = pl.BlockSpec(memory_space=pl.ANY)
+    coords_block, masses_block = (3, REGION, BLOCK), (REGION, BLOCK)
+
+    def region_of(g):
+        return lax.rem(g + SWAPS, regions)
+
+    sums, turned = pl.pallas_call(
         moments_kernel,
-        grid=(stays,),
-        in_specs=[
-            pl.BlockSpec(coords_block, lambda g: (0, g + SWAPS, 0)),
-            pl.BlockSpec(masses_block, lambda g: (g + SWAPS, 0)),
-        ],
-        out_specs=[sums_spec, turned_spec],
-        out_shape=[
-            jax.ShapeDtypeStruct((nodes_count, stays * REGION), jnp.float32),
-            jax.ShapeDtypeStruct((3, BLOCK, stays * REGION), jnp.float32),
-        ],
-        scratch_shapes=moment_scratch(nodes_count),
-        compiler_params=params(),
-        cost_estimate=pl.CostEstimate(flops=50_000_000, bytes_accessed=4_000_000, transcendentals=0),
-    )(coords, masses)
-    whole4 = pl.BlockSpec((4, REGION, BLOCK), lambda g: (0, 0, 0))
-    swapped, swapped_turned = pl.pallas_call(
-        swapped_moments_kernel,
-        grid=(SWAPS,),
+        grid=(regions,),
         in_specs=[
             pl.BlockSpec(memory_space=pltpu.SMEM),
-            pl.BlockSpec(coords_block, lambda g: (0, g, 0)),
-            pl.BlockSpec(masses_block, lambda g: (g, 0)),
-            whole4,
-            whole4,
-            whole4,
-        ],
-        out_specs=[sums_spec, turned_spec],
+            pl.BlockSpec(coords_block, lambda g: (0, region_of(g), 0)),
+            pl.BlockSpec(masses_block, lambda g: (region_of(g), 0)),
+            hbm,
+            hbm,
+        ],
+        out_specs=[
+            pl.BlockSpec((nodes_count, REGION), lambda g: (0, region_of(g))),
+            pl.BlockSpec((3, BLOCK, REGION), lambda g: (0, 0, region_of(g))),
+        ],
         out_shape=[
-            jax.ShapeDtypeStruct((nodes_count, SWAPS * REGION), jnp.float32),
-            jax.ShapeDtypeStruct((3, BLOCK, SWAPS * REGION), jnp.float32),
-        ],
-        scratch_shapes=[pltpu.VMEM(coords_block, jnp.float32), pltpu.VMEM(masses_block, jnp.float32)]
+            jax.ShapeDtypeStruct((nodes_count, blocks), jnp.float32),
+            jax.ShapeDtypeStruct((3, BLOCK, blocks), jnp.float32),
+        ],
+        scratch_shapes=[
+            pltpu.VMEM(coords_block, jnp.float32),
+            pltpu.VMEM(masses_block, jnp.float32),
+            pltpu.VMEM((SWAPS, 4, REGION, BLOCK), jnp.float32),
+            pltpu.SemaphoreType.DMA((2 * SWAPS,)),
+            pltpu.SemaphoreType.DMA((2 * SWAPS,)),
+        ]
         + moment_scratch(nodes_count),
-        compiler_params=params(),
-    )(swap_counts.reshape(SWAPS), coords, masses, *got)
+        compiler_params=params(collective_id=1, has_side_effects=True),
+    )(swap_counts.reshape(SWAPS), coords, masses, coords, masses)
     basis = node_basis()
     exact = functools.partial(jnp.dot, precision=lax.Precision.HIGHEST, preferred_element_type=jnp.float32)
     compress_polys = exact(compress.T, basis)
@@ -469,7 +478,7 @@
     vmem = pl.BlockSpec(memory_space=pltpu.VMEM)
     own, incoming = pl.pallas_call(
         coefficients_kernel,
-        in_specs=[pl.BlockSpec(memory_space=pltpu.SMEM), vmem, vmem, vmem, vmem],
+        in_specs=[pl.BlockSpec(memory_space=pltpu.SMEM), vmem, vmem, vmem],
         out_specs=[vmem, vmem],
         out_shape=[
             jax.ShapeDtypeStruct((leaves, 2 * RANK), jnp.float32),
@@ -482,14 +491,13 @@
             pltpu.SemaphoreType.DMA,
         ],
         compiler_params=params(collective_id=0, has_side_effects=True),
-    )(send.reshape(-1), swapped, stayed, leaf_row, compress_polys)
+    )(send.reshape(-1), sums, leaf_row, compress_polys)
     local = translate(own, incoming, inter_source, inter_offset, m2l_kernels)
     values = pl.pallas_call(
         evaluate_kernel,
         grid=(regions,),
         in_specs=[
-            pl.BlockSpec((3, BLOCK, REGION), lambda g: (0, 0, jnp.minimum(g, SWAPS - 1))),
-            pl.BlockSpec((3, BLOCK, REGION), lambda g: (0, 0, jnp.maximum(g - SWAPS, 0))),
+            pl.BlockSpec((3, BLOCK, REGION), lambda g: (0, 0, g)),
             pl.BlockSpec((1, blocks), lambda g: (0, 0)),
             pl.BlockSpec((leaves, RANK), lambda g: (0, 0)),
             pl.BlockSpec((nodes_count, RANK), lambda g: (0, 0)),
@@ -497,12 +505,11 @@
         out_specs=pl.BlockSpec((REGION, BLOCK), lambda g: (g, 0)),
         out_shape=jax.ShapeDtypeStruct((blocks, BLOCK), jnp.float32),
         scratch_shapes=[
-            pltpu.VMEM((3, BLOCK, REGION), jnp.float32),
             pltpu.VMEM((regions, nodes_count, REGION), jnp.float32),
             pltpu.VMEM((BLOCK, REGION), jnp.float32),
         ],
         compiler_params=params(),
-    )(swapped_turned, stayed_turned, leaf_row, local, expand_polys)
+    )(turned, leaf_row, local, expand_polys)
     return values.reshape(local_bodies)
 
 

time: 170 us -> 165 us (0.971)
  starting transfers between devices: 6.87 us -> 0 us
  Pallas kernels: 151 us -> 156 us
  other arithmetic: 3.02 us -> 0.89 us
    ppermute x3 -> x0, starting transfers between devices: 6.87 us -> none  [from_partner(): return lax.ppermute(block, axis, route)]
    pallas_call x2 -> x1, Pallas kernels: 15.5 us -> 18.9 us  [on_device(): pl.pallas_call(moments_kernel, grid=(regions,), in_specs=[pl.BlockSpec(me...]
    pallas_call x1, Pallas kernels: 19.3 us -> 21.5 us  [on_device(): pl.pallas_call(coefficients_kernel, in_specs=[pl.BlockSpec(memory_space=p...]
    concatenate x3 -> x0, other arithmetic: 2.14 us -> none  [on_device(): jnp.concatenate([coords[:, at], masses[None, at]], axis=0)]
  transfers between devices with their start and end apart: 3 -> 0, of which waited for: 0 -> 0; matrix products, arithmetic and copies ran while one was open for 4% -> 0% of each run, Pallas kernels for 5% -> 0%
where the time goes in v5:
time: 165 us; the launch traced here: 164 us
  Pallas kernels  156 us (95%)
  local copies, waits for them, and re-layouts  5.69 us (3%)
  matrix products  1.88 us (1%)
    pallas_call x1, Pallas kernels, translate(): pl.pallas_call(functools.partial(translate_kernel, leaves, inter), grid=(...  103 us
    pallas_call x1, Pallas kernels, on_device(): pl.pallas_call(coefficients_kernel, in_specs=[pl.BlockSpec(memory_space=p...  21.5 us
    pallas_call x1, Pallas kernels, on_device(): pl.pallas_call(moments_kernel, grid=(regions,), in_specs=[pl.BlockSpec(me...  18.9 us
    pallas_call x1, Pallas kernels, on_device(): pl.pallas_call(evaluate_kernel, grid=(regions,), in_specs=[pl.BlockSpec((...  12.8 us

profile of v5, /device:TPU:1, one launch (start us, length us, event | category | flops | bytes accessed | tf_op | source)
XLA Modules:
  0.0 164.5 jit_solution(10683648125479200737)
XLA Ops:
  0.0 0.0 copy-start
  0.0 2.9 %copy.32 = f32[1,3,1024,128]{3,2,1,0:T(8,128)} copy(f32[1,3,1024,128]{3,1,2,0:T(4,128)} %bitcast.18) | data formatting | bytes 3145728
  2.9 0.0 copy-start.6
  2.9 0.0 copy-start.4
  2.9 0.0 copy-start.1
  2.9 0.0 copy-start.2
  2.9 18.9 %shard_map.118 = (f32[216,1024]{1,0:T(8,128)}, f32[3,128,1024]{2,1,0:T(8,128)}) custom-call(s32[3]{0:T(128)} %bitcast.21, f32[3,1024,128]{2,1,0:T(8,128)} %bitcast.14, f32[1024,128]{1,0:T(8,128)} %bitcast.16, f32[3,1024,128]{2,1,0:T(8,128)} %bitcast.15, f32[1024,128]{1,0:T(8,128)} %bitcast.17), custom_call_target="tpu_custom_call" | custom-call | tf_op jit(solution)/shard_map/pallas_call | solution.py:444
  21.8 0.0 copy-done.6
  21.8 0.1 copy.26
  21.9 0.1 add.66
  22.0 0.1 sub.33
  22.1 0.6 sub.34.send_ref
  22.7 0.0 copy-done
  22.7 0.0 copy-done.4
  22.7 0.9 convolution_bitcast_fusion.compress_ref
  23.6 21.5 %shard_map.119 = (f32[640,128]{1,0:T(8,128)}, bf16[2048,128]{1,0:T(8,128)(2,1)}) custom-call(s32[4096]{0:T(1024)} %sub.34.send_ref, f32[216,1024]{1,0:T(8,128)} %get-tuple-element.10.sums_ref, s32[1,1024]{1,0:T(1,128)} %bitcast.19, f32[64,216]{1,0:T(8,128)} %convolution_bitcast_fusion.compress_ref), custom_call_target="tpu_custom_call" | custom-call | tf_op jit(solution)/shard_map/pallas_call | solution.py:479
  45.1 0.0 copy-done.1
  45.1 0.0 copy-done.2
  45.1 0.2 broadcast_shift-right-arithmetic_fusion
  45.3 0.2 copy.25
  45.6 0.9 pad.9.off_ref
  46.5 0.2 copy.29
  46.8 1.1 reshape.97.src_ref
  48.0 0.0 copy-start.3
  48.0 0.0 copy-start.5
  48.0 102.7 %shard_map.120.local_ref = f32[640,64]{1,0:T(8,128)} custom-call(s32[122880]{0:T(1024)} %reshape.97.src_ref, f32[640,256]{1,0:T(8,128)} %pad.9.off_ref, f32[640,128]{1,0:T(8,128)} %get-tuple-element.11.own_ref, bf16[2048,128]{1,0:T(8,128)(2,1)} %get-tuple-element.12.ghost_ref, bf16[64,20224]{1,0:T(8,128)(2,1)} %kernels_ref.1), custom_call_target="tpu_custom_call" | custom-call | tf_op jit(solution)/shard_map/pallas_call | solution.py:353
  150.7 0.0 copy-done.3
  150.7 0.0 copy-done.5
  150.7 1.0 fusion.1.expand_ref
  151.7 12.8 %shard_map.121 = f32[1024,128]{1,0:T(8,128)} custom-call(f32[3,128,1024]{2,1,0:T(8,128)} %get-tuple-element.9.turned_ref, s32[1,1024]{1,0:T(1,128)} %bitcast.20, f32[640,64]{1,0:T(8,128)} %shard_map.120.local_ref, f32[216,64]{1,0:T(8,128)} %fusion.1.expand_ref), custom_call_target="tpu_custom_call" | custom-call | tf_op jit(solution)/shard_map/pallas_call | solution.py:496
  (6 shorter events, 0.1 us)
Async XLA Ops:
  0.0 22.7 %copy-start = (f32[216,64]{0,1:T(8,128)S(1)}, f32[216,64]{0,1:T(8,128)}, u32[]{:S(2)}) copy-start(f32[216,64]{0,1:T(8,128)} %param.19) | copy-start | bytes 165892
  2.9 18.9 %copy-start.6 = (s32[1,128,32]{1,2,0:T(8,128)S(1)}, s32[1,128,32]{1,2,0:T(8,128)}, u32[]{:S(2)}) copy-start(s32[1,128,32]{1,2,0:T(8,128)} %param.16) | copy-start | bytes 49156
  2.9 19.8 %copy-start.4 = (f32[216,216]{1,0:T(8,128)S(1)}, f32[216,216]{1,0:T(8,128)}, u32[]{:S(2)}) copy-start(f32[216,216]{1,0:T(8,128)} %constant.58.clone) | copy-start | bytes 559876
  2.9 42.2 %copy-start.1 = (s32[640,189]{0,1:T(8,128)S(1)}, s32[640,189]{0,1:T(8,128)}, u32[]{:S(2)}) copy-start(s32[640,189]{0,1:T(8,128)} %param.18) | copy-start | bytes 1451524
  2.9 42.2 %copy-start.2 = (s32[640,189]{0,1:T(8,128)S(1)}, s32[640,189]{0,1:T(8,128)}, u32[]{:S(2)}) copy-start(s32[640,189]{0,1:T(8,128)} %param.17) | copy-start | bytes 1451524
  48.0 102.7 %copy-start.3 = (f32[216,216]{1,0:T(8,128)S(1)}, f32[216,216]{1,0:T(8,128)}, u32[]{:S(2)}) copy-start(f32[216,216]{1,0:T(8,128)} %constant.59.clone) | copy-start | bytes 559876
  48.0 102.7 %copy-start.5 = (f32[64,216]{1,0:T(8,128)S(1)}, f32[64,216]{1,0:T(8,128)}, u32[]{:S(2)}) copy-start(f32[64,216]{1,0:T(8,128)} %param.21) | copy-start | bytes 165892

commit v6 on v5

--- a/solution.py
+++ b/solution.py
@@ -19,6 +19,7 @@
 PITCH = 81
 UNROLL = 8
 STRIDE = 9
+BATCH = 4
 
 
 def params(**more):
@@ -170,7 +171,23 @@
 
 
 def coefficients_kernel(
-    send_ref, sums_ref, leaf_ref, compress_ref, own_ref, got_ref, padded, packed, send_sem, recv_sem
+    send_ref,
+    sums_ref,
+    leaf_ref,
+    compress_ref,
+    expand_ref,
+    basis_ref,
+    source_ref,
+    offset_ref,
+    own_ref,
+    got_ref,
+    polys_ref,
+    row_ref,
+    pair_ref,
+    padded,
+    packed,
+    send_sem,
+    recv_sem,
 ):
     leaves = own_ref.shape[0]
     peers = got_ref.shape[0] // 16
@@ -188,9 +205,11 @@
     lax.fori_loop(1, peers, greet, 0)
     onehot = lax.broadcasted_iota(jnp.int32, (leaves, leaf_ref.shape[1]), 0) == leaf_ref[...]
     onehot = jnp.where(onehot, 1.0, 0.0).astype(jnp.bfloat16)
-    moved = jnp.dot(
-        compress_ref[...], sums_ref[...], precision=lax.Precision.HIGHEST, preferred_element_type=jnp.float32
+    exact = functools.partial(
+        lax.dot_general, precision=lax.Precision.HIGHEST, preferred_element_type=jnp.float32
     )
+    compress = exact(compress_ref[...], basis_ref[...], (((1,), (0,)), ((), ())))
+    moved = exact(compress, sums_ref[...], (((1,), (0,)), ((), ())))
     both = jnp.concatenate(split_two(moved), axis=0)
     total = lax.dot_general(onehot, both, (((1,), (1,)), ((), ())), preferred_element_type=jnp.float32)
     own = (total + pltpu.roll(total, RANK, 1)).astype(jnp.bfloat16).astype(jnp.float32)
@@ -213,24 +232,45 @@
             halves.append(rows)
         return jnp.concatenate(halves, axis=0).astype(jnp.bfloat16)
 
-    def send(hop, carry):
-        peer = lax.rem(me + hop, peers)
-        at = pl.ds(pl.multiple_of(peer * 16, 16), 16)
-        packed[at, :] = pack(peer)
-        pltpu.make_async_remote_copy(
-            src_ref=packed.at[at, :],
-            dst_ref=got_ref.at[mine, :],
-            send_sem=send_sem,
-            recv_sem=recv_sem,
-            device_id=(peer // subs, lax.rem(peer, subs)),
-            device_id_type=pl.DeviceIdType.MESH,
-        ).start()
+    def send(hops):
+        rows = [lax.rem(me + hop, peers) for hop in hops]
+        for peer in rows:
+            packed[pl.ds(pl.multiple_of(peer * 16, 16), 16), :] = pack(peer)
+        for peer in rows:
+            pltpu.make_async_remote_copy(
+                src_ref=packed.at[pl.ds(pl.multiple_of(peer * 16, 16), 16), :],
+                dst_ref=got_ref.at[mine, :],
+                send_sem=send_sem,
+                recv_sem=recv_sem,
+                device_id=(peer // subs, lax.rem(peer, subs)),
+                device_id_type=pl.DeviceIdType.MESH,
+            ).start()
+
+    def send_batch(batch, carry):
+        send([1 + batch * BATCH + k for k in range(BATCH)])
         return carry
 
     mine = pl.ds(pl.multiple_of(me * 16, 16), 16)
     got_ref[mine, :] = pack(me)
     pl.semaphore_wait(barrier, peers - 1)
-    lax.fori_loop(1, peers, send, 0)
+    batches = (peers - 1) // BATCH
+    lax.fori_loop(0, batches, send_batch, 0)
+    if batches * BATCH < peers - 1:
+        send(range(1 + batches * BATCH, peers))
+
+    polys_ref[...] = exact(basis_ref[...], expand_ref[...], (((0,), (0,)), ((), ())))
+    inter = source_ref.shape[1]
+    ghosts = got_ref.shape[0]
+    rows = leaves + 2 * ghosts
+    sources, offsets = source_ref[...], offset_ref[...]
+    remote = sources - leaves
+    row = leaves + lax.shift_right_arithmetic(remote, 1) + (remote & 1) * ghosts
+    row = jnp.where(remote < 0, sources, row) + (offsets & 1) * rows
+    row_ref[...] = jnp.zeros_like(row_ref)
+    row_ref[:, :inter] = row + 8 - lax.rem(lax.broadcasted_iota(jnp.int32, row.shape, 1), 8)
+    pair_ref[...] = jnp.full_like(pair_ref, -1.0)
+    pair_ref[:, :inter] = lax.shift_right_arithmetic(offsets, 1).astype(jnp.float32)
+
     others = pl.ds(0, (peers - 1) * 16)
     everything = pltpu.make_async_remote_copy(
         src_ref=packed.at[others, :],
@@ -339,16 +379,10 @@
         lax.fori_loop(0, GROUP // UNROLL, body, 0)
 
 
-def translate(own, ghost, sources, offsets, m2l_kernels):
-    leaves, inter = sources.shape
+def translate(own, ghost, row, pair, inter, m2l_kernels):
+    leaves = own.shape[0]
     ghosts = ghost.shape[0]
     rows = leaves + 2 * ghosts
-    remote = sources - leaves
-    row = jnp.where(remote < 0, sources, leaves + lax.shift_right_arithmetic(remote, 1) + (remote & 1) * ghosts)
-    row = row + (offsets & 1) * rows
-    row = row + 8 - jnp.arange(inter, dtype=jnp.int32)[None, :] % 8
-    row = jnp.pad(row, ((0, 0), (0, SLOTS - inter))).reshape(-1)
-    pair = jnp.pad((offsets >> 1).astype(jnp.float32), ((0, 0), (0, 256 - inter)), constant_values=-1.0)
     steps = leaves // GROUP
     return pl.pallas_call(
         functools.partial(translate_kernel, leaves, inter),
@@ -371,7 +405,7 @@
             pltpu.SemaphoreType.DMA,
         ],
         compiler_params=params(),
-    )(row, pair, own, ghost, m2l_kernels)
+    )(row.reshape(-1), pair, own, ghost, m2l_kernels)
 
 
 def evaluate_kernel(turned_ref, leaf_ref, local_ref, expand_ref, out_ref, nodes, result):
@@ -469,20 +503,19 @@
         + moment_scratch(nodes_count),
         compiler_params=params(collective_id=1, has_side_effects=True),
     )(swap_counts.reshape(SWAPS), coords, masses, coords, masses)
-    basis = node_basis()
-    exact = functools.partial(jnp.dot, precision=lax.Precision.HIGHEST, preferred_element_type=jnp.float32)
-    compress_polys = exact(compress.T, basis)
-    expand_polys = exact(basis.T, expand.T)
     leaf_row = leaf_of_block.reshape(1, blocks)
     send = let_send.reshape(peers, per_peer) + 8 - (jnp.arange(per_peer, dtype=jnp.int32)[None, :] // 2) % 8
     vmem = pl.BlockSpec(memory_space=pltpu.VMEM)
-    own, incoming = pl.pallas_call(
+    own, incoming, expand_polys, row, pair = pl.pallas_call(
         coefficients_kernel,
-        in_specs=[pl.BlockSpec(memory_space=pltpu.SMEM), vmem, vmem, vmem],
-        out_specs=[vmem, vmem],
+        in_specs=[pl.BlockSpec(memory_space=pltpu.SMEM)] + [vmem] * 7,
+        out_specs=[vmem] * 5,
         out_shape=[
             jax.ShapeDtypeStruct((leaves, 2 * RANK), jnp.float32),
             jax.ShapeDtypeStruct((peers * per_peer // 2, 2 * RANK), jnp.bfloat16),
+            jax.ShapeDtypeStruct((nodes_count, RANK), jnp.float32),
+            jax.ShapeDtypeStruct((leaves, SLOTS), jnp.int32),
+            jax.ShapeDtypeStruct((leaves, 256), jnp.float32),
         ],
         scratch_shapes=[
             pltpu.VMEM((leaves + 16, 2 * RANK), jnp.float32),
@@ -491,8 +524,8 @@
             pltpu.SemaphoreType.DMA,
         ],
         compiler_params=params(collective_id=0, has_side_effects=True),
-    )(send.reshape(-1), sums, leaf_row, compress_polys)
-    local = translate(own, incoming, inter_source, inter_offset, m2l_kernels)
+    )(send.reshape(-1), sums, leaf_row, compress.T, expand.T, node_basis(), inter_source, inter_offset)
+    local = translate(own, incoming, row, pair, inter_source.shape[1], m2l_kernels)
     values = pl.pallas_call(
         evaluate_kernel,
         grid=(regions,),

time: 165 us -> 167 us (1.012)
  local copies, waits for them, and re-layouts: 5.69 us -> 9.51 us
  matrix products: 1.88 us -> 0 us
    unnamed x16 -> x6, local copies, waits for them, and re-layouts: 3.12 us -> 7.05 us
    dot_general x2 -> x0, matrix products: 1.88 us -> none  [the longest x1 0.99 us: on_device(): expand_polys = exact(basis.T, expand.T)]
where the time goes in v6:
time: 167 us
  Pallas kernels  156 us (93%)
  local copies, waits for them, and re-layouts  9.51 us (6%)
    pallas_call x1, Pallas kernels, translate(): pl.pallas_call(functools.partial(translate_kernel, leaves, inter), grid=(...  103 us
    pallas_call x1, Pallas kernels, on_device(): pl.pallas_call(coefficients_kernel, in_specs=[pl.BlockSpec(memory_space=p...  21.9 us
    pallas_call x1, Pallas kernels, on_device(): pl.pallas_call(moments_kernel, grid=(regions,), in_specs=[pl.BlockSpec(me...  18.6 us
    pallas_call x1, Pallas kernels, on_device(): pl.pallas_call(evaluate_kernel, grid=(regions,), in_specs=[pl.BlockSpec((...  12.8 us
    unnamed x6, local copies, waits for them, and re-layouts  7.05 us

profile of v6, /device:TPU:1, one launch (start us, length us, event | category | flops | bytes accessed | tf_op | source)
XLA Modules:
  0.0 166.9 jit_solution(11490640030409897434)
XLA Ops:
  0.0 0.0 copy-start
  0.0 0.9 broadcast_add_fusion
  0.9 0.1 copy.15
  1.0 0.1 add.29
  1.1 0.1 sub.19
  1.1 0.6 sub.20.send_ref
  1.8 1.6 copy.16
  3.3 2.1 %copy.17.source_ref = s32[640,189]{1,0:T(8,128)} copy(s32[640,189]{0,1:T(8,128)} %param.16) | data formatting | bytes 967680 | tf_op args[5]
  5.5 2.1 %copy.18.offset_ref = s32[640,189]{1,0:T(8,128)} copy(s32[640,189]{0,1:T(8,128)} %param.17) | data formatting | bytes 967680 | tf_op args[6]
  7.6 0.0 copy-done
  7.6 1.2 copy.21
  8.8 18.6 %shard_map.109 = (f32[216,1024]{1,0:T(8,128)}, f32[3,128,1024]{2,1,0:T(8,128)}) custom-call(s32[3]{0:T(128)} %bitcast.19, f32[3,1024,128]{2,1,0:T(8,128)} %bitcast.10, f32[1024,128]{1,0:T(8,128)} %bitcast.12, f32[3,1024,128]{2,1,0:T(8,128)} %bitcast.11, f32[1024,128]{1,0:T(8,128)} %bitcast.13), custom_call_target="tpu_custom_call" | custom-call | tf_op jit(solution)/shard_map/pallas_call | solution.py:478
  27.4 21.9 %shard_map.110 = (f32[640,128]{1,0:T(8,128)}, bf16[2048,128]{1,0:T(8,128)(2,1)}, f32[216,64]{1,0:T(8,128)}, s32[640,192]{1,0:T(8,128)}, f32[640,256]{1,0:T(8,128)}) custom-call(s32[4096]{0:T(1024)} %sub.20.send_ref, f32[216,1024]{1,0:T(8,128)} %get-tuple-element.13.sums_ref, s32[1,1024]{1,0:T(1,128)} %bitcast.17, f32[64,216]{1,0:T(8,128)} %bitcast.16, ...), custom_call_target="tpu_custom_call" | custom-call | tf_op jit(solution)/shard_map/pallas_call | solution.py:509
  49.4 2.2 %reshape.82.src_ref = s32[122880]{0:T(1024)} reshape(s32[640,192]{1,0:T(8,128)} %get-tuple-element.14) | data formatting | bytes 983040 | tf_op jit(solution)/shard_map/reshape | solution.py:408
  51.6 102.5 %shard_map.111.local_ref = f32[640,64]{1,0:T(8,128)} custom-call(s32[122880]{0:T(1024)} %reshape.82.src_ref, f32[640,256]{1,0:T(8,128)} %get-tuple-element.15.off_ref, f32[640,128]{1,0:T(8,128)} %get-tuple-element.16.own_ref, bf16[2048,128]{1,0:T(8,128)(2,1)} %get-tuple-element.17.ghost_ref, bf16[64,20224]{1,0:T(8,128)(2,1)} %kernels_ref.1), custom_call_target="tpu_custom_call" | custom-call | tf_op jit(solution)/shard_map/pallas_call | solution.py:387
  154.1 12.8 %shard_map.112 = f32[1024,128]{1,0:T(8,128)} custom-call(f32[3,128,1024]{2,1,0:T(8,128)} %get-tuple-element.12.turned_ref, s32[1,1024]{1,0:T(1,128)} %bitcast.18, f32[640,64]{1,0:T(8,128)} %shard_map.111.local_ref, f32[216,64]{1,0:T(8,128)} %get-tuple-element.18.expand_ref), custom_call_target="tpu_custom_call" | custom-call | tf_op jit(solution)/shard_map/pallas_call | solution.py:529
  (2 shorter events, 0.0 us)
Async XLA Ops:
  0.0 7.6 %copy-start = (f32[3,131072]{1,0:T(4,128)S(1)}, f32[3,131072]{1,0:T(4,128)}, u32[]{:S(2)}) copy-start(f32[3,131072]{1,0:T(4,128)} %param.11) | copy-start | bytes 4718596

commit v7 on v5

--- a/solution.py
+++ b/solution.py
@@ -19,6 +19,7 @@
 PITCH = 81
 UNROLL = 8
 STRIDE = 9
+BATCH = 4
 
 
 def params(**more):
@@ -213,24 +214,31 @@
             halves.append(rows)
         return jnp.concatenate(halves, axis=0).astype(jnp.bfloat16)
 
-    def send(hop, carry):
-        peer = lax.rem(me + hop, peers)
-        at = pl.ds(pl.multiple_of(peer * 16, 16), 16)
-        packed[at, :] = pack(peer)
-        pltpu.make_async_remote_copy(
-            src_ref=packed.at[at, :],
-            dst_ref=got_ref.at[mine, :],
-            send_sem=send_sem,
-            recv_sem=recv_sem,
-            device_id=(peer // subs, lax.rem(peer, subs)),
-            device_id_type=pl.DeviceIdType.MESH,
-        ).start()
+    def send(hops):
+        rows = [lax.rem(me + hop, peers) for hop in hops]
+        for peer in rows:
+            packed[pl.ds(pl.multiple_of(peer * 16, 16), 16), :] = pack(peer)
+        for peer in rows:
+            pltpu.make_async_remote_copy(
+                src_ref=packed.at[pl.ds(pl.multiple_of(peer * 16, 16), 16), :],
+                dst_ref=got_ref.at[mine, :],
+                send_sem=send_sem,
+                recv_sem=recv_sem,
+                device_id=(peer // subs, lax.rem(peer, subs)),
+                device_id_type=pl.DeviceIdType.MESH,
+            ).start()
+
+    def send_batch(batch, carry):
+        send([1 + batch * BATCH + k for k in range(BATCH)])
         return carry
 
     mine = pl.ds(pl.multiple_of(me * 16, 16), 16)
     got_ref[mine, :] = pack(me)
     pl.semaphore_wait(barrier, peers - 1)
-    lax.fori_loop(1, peers, send, 0)
+    batches = (peers - 1) // BATCH
+    lax.fori_loop(0, batches, send_batch, 0)
+    if batches * BATCH < peers - 1:
+        send(range(1 + batches * BATCH, peers))
     others = pl.ds(0, (peers - 1) * 16)
     everything = pltpu.make_async_remote_copy(
         src_ref=packed.at[others, :],

time: 165 us -> 164 us (level)
  no operation moved by 1% of the time
where the time goes in v7:
time: 164 us
  Pallas kernels  155 us (95%)
  local copies, waits for them, and re-layouts  5.69 us (3%)
  matrix products  1.88 us (1%)
    pallas_call x1, Pallas kernels, translate(): pl.pallas_call(functools.partial(translate_kernel, leaves, inter), grid=(...  103 us
    pallas_call x1, Pallas kernels, on_device(): pl.pallas_call(coefficients_kernel, in_specs=[pl.BlockSpec(memory_space=p...  20.9 us
    pallas_call x1, Pallas kernels, on_device(): pl.pallas_call(moments_kernel, grid=(regions,), in_specs=[pl.BlockSpec(me...  18.9 us
    pallas_call x1, Pallas kernels, on_device(): pl.pallas_call(evaluate_kernel, grid=(regions,), in_specs=[pl.BlockSpec((...  12.8 us

profile of v7, /device:TPU:1, one launch (start us, length us, event | category | flops | bytes accessed | tf_op | source)
XLA Modules:
  0.0 163.8 jit_solution(10179979883545176432)
XLA Ops:
  0.0 0.0 copy-start
  0.0 2.9 %copy.32 = f32[1,3,1024,128]{3,2,1,0:T(8,128)} copy(f32[1,3,1024,128]{3,1,2,0:T(4,128)} %bitcast.18) | data formatting | bytes 3145728
  2.9 0.0 copy-start.6
  2.9 0.0 copy-start.4
  2.9 0.0 copy-start.1
  2.9 0.0 copy-start.2
  2.9 18.9 %shard_map.118 = (f32[216,1024]{1,0:T(8,128)}, f32[3,128,1024]{2,1,0:T(8,128)}) custom-call(s32[3]{0:T(128)} %bitcast.21, f32[3,1024,128]{2,1,0:T(8,128)} %bitcast.14, f32[1024,128]{1,0:T(8,128)} %bitcast.16, f32[3,1024,128]{2,1,0:T(8,128)} %bitcast.15, f32[1024,128]{1,0:T(8,128)} %bitcast.17), custom_call_target="tpu_custom_call" | custom-call | tf_op jit(solution)/shard_map/pallas_call | solution.py:452
  21.8 0.0 copy-done.6
  21.8 0.1 copy.26
  21.9 0.1 add.66
  22.0 0.1 sub.33
  22.1 0.6 sub.34.send_ref
  22.7 0.0 copy-done
  22.7 0.0 copy-done.4
  22.7 0.9 convolution_bitcast_fusion.compress_ref
  23.6 20.9 %shard_map.119 = (f32[640,128]{1,0:T(8,128)}, bf16[2048,128]{1,0:T(8,128)(2,1)}) custom-call(s32[4096]{0:T(1024)} %sub.34.send_ref, f32[216,1024]{1,0:T(8,128)} %get-tuple-element.10.sums_ref, s32[1,1024]{1,0:T(1,128)} %bitcast.19, f32[64,216]{1,0:T(8,128)} %convolution_bitcast_fusion.compress_ref), custom_call_target="tpu_custom_call" | custom-call | tf_op jit(solution)/shard_map/pallas_call | solution.py:487
  44.5 0.0 copy-done.1
  44.5 0.0 copy-done.2
  44.5 0.2 broadcast_shift-right-arithmetic_fusion
  44.8 0.2 copy.25
  45.0 0.9 pad.9.off_ref
  45.9 0.2 copy.29
  46.2 1.1 reshape.97.src_ref
  47.4 0.0 copy-start.3
  47.4 0.0 copy-start.5
  47.4 102.6 %shard_map.120.local_ref = f32[640,64]{1,0:T(8,128)} custom-call(s32[122880]{0:T(1024)} %reshape.97.src_ref, f32[640,256]{1,0:T(8,128)} %pad.9.off_ref, f32[640,128]{1,0:T(8,128)} %get-tuple-element.11.own_ref, bf16[2048,128]{1,0:T(8,128)(2,1)} %get-tuple-element.12.ghost_ref, bf16[64,20224]{1,0:T(8,128)(2,1)} %kernels_ref.1), custom_call_target="tpu_custom_call" | custom-call | tf_op jit(solution)/shard_map/pallas_call | solution.py:361
  150.0 0.0 copy-done.3
  150.0 0.0 copy-done.5
  150.0 1.0 fusion.1.expand_ref
  151.0 12.8 %shard_map.121 = f32[1024,128]{1,0:T(8,128)} custom-call(f32[3,128,1024]{2,1,0:T(8,128)} %get-tuple-element.9.turned_ref, s32[1,1024]{1,0:T(1,128)} %bitcast.20, f32[640,64]{1,0:T(8,128)} %shard_map.120.local_ref, f32[216,64]{1,0:T(8,128)} %fusion.1.expand_ref), custom_call_target="tpu_custom_call" | custom-call | tf_op jit(solution)/shard_map/pallas_call | solution.py:504
  (6 shorter events, 0.1 us)
Async XLA Ops:
  0.0 22.7 %copy-start = (f32[216,64]{0,1:T(8,128)S(1)}, f32[216,64]{0,1:T(8,128)}, u32[]{:S(2)}) copy-start(f32[216,64]{0,1:T(8,128)} %param.19) | copy-start | bytes 165892
  2.9 18.9 %copy-start.6 = (s32[1,128,32]{1,2,0:T(8,128)S(1)}, s32[1,128,32]{1,2,0:T(8,128)}, u32[]{:S(2)}) copy-start(s32[1,128,32]{1,2,0:T(8,128)} %param.16) | copy-start | bytes 49156
  2.9 19.8 %copy-start.4 = (f32[216,216]{1,0:T(8,128)S(1)}, f32[216,216]{1,0:T(8,128)}, u32[]{:S(2)}) copy-start(f32[216,216]{1,0:T(8,128)} %constant.58.clone) | copy-start | bytes 559876
  2.9 41.6 %copy-start.1 = (s32[640,189]{0,1:T(8,128)S(1)}, s32[640,189]{0,1:T(8,128)}, u32[]{:S(2)}) copy-start(s32[640,189]{0,1:T(8,128)} %param.18) | copy-start | bytes 1451524
  2.9 41.6 %copy-start.2 = (s32[640,189]{0,1:T(8,128)S(1)}, s32[640,189]{0,1:T(8,128)}, u32[]{:S(2)}) copy-start(s32[640,189]{0,1:T(8,128)} %param.17) | copy-start | bytes 1451524
  47.4 102.6 %copy-start.3 = (f32[216,216]{1,0:T(8,128)S(1)}, f32[216,216]{1,0:T(8,128)}, u32[]{:S(2)}) copy-start(f32[216,216]{1,0:T(8,128)} %constant.59.clone) | copy-start | bytes 559876
  47.4 102.6 %copy-start.5 = (f32[64,216]{1,0:T(8,128)S(1)}, f32[64,216]{1,0:T(8,128)}, u32[]{:S(2)}) copy-start(f32[64,216]{1,0:T(8,128)} %param.21) | copy-start | bytes 165892

commit v8 on v7

--- a/solution.py
+++ b/solution.py
@@ -403,24 +403,28 @@
             nodes[2 * pair] = values[:, :REGION]
             nodes[2 * pair + 1] = values[:, REGION:]
 
-    def chunk(v, carry):
-        at = pl.ds(pl.multiple_of(v * 16, 16), 16)
-        px, py, pz = (chebyshev(turned_ref[dim, at, :]) for dim in range(3))
-        value = None
-        for i in range(ORDER):
-            middle = None
-            for j in range(ORDER):
-                first = (i * ORDER + j) * ORDER
-                inner = nodes[step, pl.ds(first + 1, 1), :] * pz[0] + nodes[step, pl.ds(first, 1), :]
-                for k in range(2, ORDER):
-                    inner += nodes[step, pl.ds(first + k, 1), :] * pz[k - 1]
-                middle = inner if j == 0 else middle + inner * py[j - 1]
-            value = middle if i == 0 else value + middle * px[i - 1]
-        result[at, :] = value
-        return carry
-
-    lax.fori_loop(0, BLOCK // 16, chunk, 0)
-    out_ref[...] = result[...].T
+    for half in range(2):
+        lanes = slice(half * REGION, (half + 1) * REGION)
+        region = 2 * step + half
+
+        def chunk(v, carry):
+            at = pl.ds(pl.multiple_of(v * 16, 16), 16)
+            px, py, pz = (chebyshev(turned_ref[dim, at, lanes]) for dim in range(3))
+            value = None
+            for i in range(ORDER):
+                middle = None
+                for j in range(ORDER):
+                    first = (i * ORDER + j) * ORDER
+                    inner = nodes[region, pl.ds(first + 1, 1), :] * pz[0] + nodes[region, pl.ds(first, 1), :]
+                    for k in range(2, ORDER):
+                        inner += nodes[region, pl.ds(first + k, 1), :] * pz[k - 1]
+                    middle = inner if j == 0 else middle + inner * py[j - 1]
+                value = middle if i == 0 else value + middle * px[i - 1]
+            result[at, :] = value
+            return carry
+
+        lax.fori_loop(0, BLOCK // 16, chunk, 0)
+        out_ref[lanes, :] = result[...].T
 
 
 def on_device(
@@ -503,14 +507,14 @@
     local = translate(own, incoming, inter_source, inter_offset, m2l_kernels)
     values = pl.pallas_call(
         evaluate_kernel,
-        grid=(regions,),
+        grid=(regions // 2,),
         in_specs=[
-            pl.BlockSpec((3, BLOCK, REGION), lambda g: (0, 0, g)),
+            pl.BlockSpec((3, BLOCK, 2 * REGION), lambda g: (0, 0, g)),
             pl.BlockSpec((1, blocks), lambda g: (0, 0)),
             pl.BlockSpec((leaves, RANK), lambda g: (0, 0)),
             pl.BlockSpec((nodes_count, RANK), lambda g: (0, 0)),
         ],
-        out_specs=pl.BlockSpec((REGION, BLOCK), lambda g: (g, 0)),
+        out_specs=pl.BlockSpec((2 * REGION, BLOCK), lambda g: (g, 0)),
         out_shape=jax.ShapeDtypeStruct((blocks, BLOCK), jnp.float32),
         scratch_shapes=[
             pltpu.VMEM((regions, nodes_count, REGION), jnp.float32),

time: 164 us -> 164 us (level)
  no operation moved by 1% of the time
where the time goes in v8:
time: 164 us
  Pallas kernels  155 us (95%)
  local copies, waits for them, and re-layouts  5.69 us (3%)
  matrix products  1.87 us (1%)
    pallas_call x1, Pallas kernels, translate(): pl.pallas_call(functools.partial(translate_kernel, leaves, inter), grid=(...  103 us
    pallas_call x1, Pallas kernels, on_device(): pl.pallas_call(coefficients_kernel, in_specs=[pl.BlockSpec(memory_space=p...  20.9 us
    pallas_call x1, Pallas kernels, on_device(): pl.pallas_call(moments_kernel, grid=(regions,), in_specs=[pl.BlockSpec(me...  18.9 us
    pallas_call x1, Pallas kernels, on_device(): pl.pallas_call(evaluate_kernel, grid=(regions // 2,), in_specs=[pl.BlockS...  12.7 us

profile of v8, /device:TPU:1, one launch (start us, length us, event | category | flops | bytes accessed | tf_op | source)
XLA Modules:
  0.0 163.7 jit_solution(6211248975848131)
XLA Ops:
  0.0 0.0 copy-start
  0.0 2.9 %copy.32 = f32[1,3,1024,128]{3,2,1,0:T(8,128)} copy(f32[1,3,1024,128]{3,1,2,0:T(4,128)} %bitcast.18) | data formatting | bytes 3145728
  2.9 0.0 copy-start.6
  2.9 0.0 copy-start.4
  2.9 0.0 copy-start.1
  2.9 0.0 copy-start.2
  2.9 18.9 %shard_map.118 = (f32[216,1024]{1,0:T(8,128)}, f32[3,128,1024]{2,1,0:T(8,128)}) custom-call(s32[3]{0:T(128)} %bitcast.21, f32[3,1024,128]{2,1,0:T(8,128)} %bitcast.14, f32[1024,128]{1,0:T(8,128)} %bitcast.16, f32[3,1024,128]{2,1,0:T(8,128)} %bitcast.15, f32[1024,128]{1,0:T(8,128)} %bitcast.17), custom_call_target="tpu_custom_call" | custom-call | tf_op jit(solution)/shard_map/pallas_call | solution.py:456
  21.8 0.0 copy-done.6
  21.8 0.1 copy.26
  21.9 0.1 add.66
  22.0 0.1 sub.33
  22.1 0.6 sub.34.send_ref
  22.7 0.0 copy-done
  22.7 0.0 copy-done.4
  22.7 0.9 convolution_bitcast_fusion.compress_ref
  23.6 20.9 %shard_map.119 = (f32[640,128]{1,0:T(8,128)}, bf16[2048,128]{1,0:T(8,128)(2,1)}) custom-call(s32[4096]{0:T(1024)} %sub.34.send_ref, f32[216,1024]{1,0:T(8,128)} %get-tuple-element.10.sums_ref, s32[1,1024]{1,0:T(1,128)} %bitcast.19, f32[64,216]{1,0:T(8,128)} %convolution_bitcast_fusion.compress_ref), custom_call_target="tpu_custom_call" | custom-call | tf_op jit(solution)/shard_map/pallas_call | solution.py:491
  44.5 0.0 copy-done.1
  44.5 0.0 copy-done.2
  44.5 0.2 broadcast_shift-right-arithmetic_fusion
  44.8 0.2 copy.25
  45.0 0.9 pad.9.off_ref
  45.9 0.2 copy.29
  46.2 1.1 reshape.97.src_ref
  47.4 0.0 copy-start.3
  47.4 0.0 copy-start.5
  47.4 102.6 %shard_map.120.local_ref = f32[640,64]{1,0:T(8,128)} custom-call(s32[122880]{0:T(1024)} %reshape.97.src_ref, f32[640,256]{1,0:T(8,128)} %pad.9.off_ref, f32[640,128]{1,0:T(8,128)} %get-tuple-element.11.own_ref, bf16[2048,128]{1,0:T(8,128)(2,1)} %get-tuple-element.12.ghost_ref, bf16[64,20224]{1,0:T(8,128)(2,1)} %kernels_ref.1), custom_call_target="tpu_custom_call" | custom-call | tf_op jit(solution)/shard_map/pallas_call | solution.py:361
  150.0 0.0 copy-done.3
  150.0 0.0 copy-done.5
  150.0 1.0 fusion.1.expand_ref
  151.0 12.7 %shard_map.121 = f32[1024,128]{1,0:T(8,128)} custom-call(f32[3,128,1024]{2,1,0:T(8,128)} %get-tuple-element.9.turned_ref, s32[1,1024]{1,0:T(1,128)} %bitcast.20, f32[640,64]{1,0:T(8,128)} %shard_map.120.local_ref, f32[216,64]{1,0:T(8,128)} %fusion.1.expand_ref), custom_call_target="tpu_custom_call" | custom-call | tf_op jit(solution)/shard_map/pallas_call | solution.py:508
  (6 shorter events, 0.1 us)
Async XLA Ops:
  0.0 22.7 %copy-start = (f32[216,64]{0,1:T(8,128)S(1)}, f32[216,64]{0,1:T(8,128)}, u32[]{:S(2)}) copy-start(f32[216,64]{0,1:T(8,128)} %param.19) | copy-start | bytes 165892
  2.9 18.9 %copy-start.6 = (s32[1,128,32]{1,2,0:T(8,128)S(1)}, s32[1,128,32]{1,2,0:T(8,128)}, u32[]{:S(2)}) copy-start(s32[1,128,32]{1,2,0:T(8,128)} %param.16) | copy-start | bytes 49156
  2.9 19.8 %copy-start.4 = (f32[216,216]{1,0:T(8,128)S(1)}, f32[216,216]{1,0:T(8,128)}, u32[]{:S(2)}) copy-start(f32[216,216]{1,0:T(8,128)} %constant.58.clone) | copy-start | bytes 559876
  2.9 41.6 %copy-start.1 = (s32[640,189]{0,1:T(8,128)S(1)}, s32[640,189]{0,1:T(8,128)}, u32[]{:S(2)}) copy-start(s32[640,189]{0,1:T(8,128)} %param.18) | copy-start | bytes 1451524
  2.9 41.6 %copy-start.2 = (s32[640,189]{0,1:T(8,128)S(1)}, s32[640,189]{0,1:T(8,128)}, u32[]{:S(2)}) copy-start(s32[640,189]{0,1:T(8,128)} %param.17) | copy-start | bytes 1451524
  47.4 102.7 %copy-start.3 = (f32[216,216]{1,0:T(8,128)S(1)}, f32[216,216]{1,0:T(8,128)}, u32[]{:S(2)}) copy-start(f32[216,216]{1,0:T(8,128)} %constant.59.clone) | copy-start | bytes 559876
  47.4 102.7 %copy-start.5 = (f32[64,216]{1,0:T(8,128)S(1)}, f32[64,216]{1,0:T(8,128)}, u32[]{:S(2)}) copy-start(f32[64,216]{1,0:T(8,128)} %param.21) | copy-start | bytes 165892
